TPU v7x, 128 devices: a whole 4x4x4 slice. The times are simulated.
128 devices in a mesh: scan: 32 (over y, x, core), cuts: 4 (over z).
Axes of the slice: x: 4, y: 4, z: 4, core: 2. Of those that a mesh axis runs over, the one named last changes fastest.
Arguments:
- probe_wave: bfloat16 [2, 512, 512], replicated, may hold values from -6 to 6
- propagator: bfloat16 [2, 512, 512], replicated
- object_slices: float32 [2, 4, 4096, 2048], P(None, 'cuts', 'scan'), may hold values from -4 to 4
- positions: int32 [64, 2], P('scan'), may hold values from 0 to 4095, as said below
- intensities: float32 [64, 512, 512], P('scan'), may hold values from 0 to 2
Outputs:
- object_gradient: float32 [2, 4, 4096, 2048], P(None, 'cuts', 'scan')
Inputs may be any that keep to these rules, and one draw needn't show every extreme that they name: `positions`: position j's row lies in [128 * (j // 2), 128 * (j // 2 + 1)); on every index of scan some position's row is the last of that range. Columns lie in 0 to 1536, both ends reached.
All inputs are finite; a program needn't handle non-finite values.
Results may differ from a plain program's by a relative error of at most 0.019.
Values may be sent and summed in bfloat16 or wider, within the bound.
A program may use at most 128 MiB of HBM per device.

v0:
```python
import math

import jax
import jax.numpy as jnp
from jax import lax
from jax.sharding import PartitionSpec as P


def passed_along(shard, axis, by):
    devices = lax.axis_size(axis)
    return lax.ppermute(shard, axis, [(i, (i + by) % devices) for i in range(devices)])


def shifted(block, axis, distance):
    devices = range(lax.axis_size(axis))
    route = [(i - distance, i) for i in devices if i - distance in devices]
    return lax.ppermute(block, axis, route)


def complex_product(left_re, left_im, right_re, right_im):
    real_part = jnp.dot(left_re, right_re, preferred_element_type=jnp.float32) - jnp.dot(
        left_im, right_im, preferred_element_type=jnp.float32
    )
    imag_part = jnp.dot(left_re, right_im, preferred_element_type=jnp.float32) + jnp.dot(
        left_im, right_re, preferred_element_type=jnp.float32
    )
    return jnp.stack([real_part, imag_part])


def dft_table(length):
    serial = jnp.arange(length, dtype=jnp.int32)
    angle_index = serial[:, None] * serial[None, :] % length
    phase_angle = angle_index.astype(jnp.float32) * (2.0 * math.pi / length)
    norm_scale = 1.0 / math.sqrt(length)
    return jnp.stack(
        [jnp.cos(phase_angle) * norm_scale, -jnp.sin(phase_angle) * norm_scale]
    ).astype(jnp.bfloat16)


def forward_section(wave_in, window, propagator):
    mixed_re = wave_in[0] * window[0] - wave_in[1] * window[1]
    mixed_im = wave_in[0] * window[1] + wave_in[1] * window[0]
    mixed = jnp.stack([mixed_re, mixed_im]).astype(jnp.bfloat16)
    halfway = complex_product(propagator[0], propagator[1], mixed[0], mixed[1]).astype(jnp.bfloat16)
    return complex_product(halfway[0], halfway[1], propagator[0].T, propagator[1].T).astype(
        jnp.bfloat16
    )


def far_gradient(exit_wave, measured, transform):
    spread = complex_product(transform[0], transform[1], exit_wave[0], exit_wave[1]).astype(
        jnp.bfloat16
    )
    farfield = complex_product(spread[0], spread[1], transform[0], transform[1])
    excess = farfield[0] * farfield[0] + farfield[1] * farfield[1] - measured
    residue = (excess[None] * farfield).astype(jnp.bfloat16)
    inverse_im = -transform[1]
    pulled = complex_product(transform[0], inverse_im, residue[0], residue[1]).astype(jnp.bfloat16)
    return complex_product(pulled[0], pulled[1], transform[0], inverse_im).astype(jnp.bfloat16)


def adjoint_section(grad_out, wave_in, window, propagator):
    conj_im = -propagator[1]
    grad_half = complex_product(grad_out[0], grad_out[1], propagator[0], conj_im).astype(
        jnp.bfloat16
    )
    grad_mixed = complex_product(propagator[0].T, conj_im.T, grad_half[0], grad_half[1])
    object_re = wave_in[0] * grad_mixed[0] + wave_in[1] * grad_mixed[1]
    object_im = wave_in[0] * grad_mixed[1] - wave_in[1] * grad_mixed[0]
    wave_re = window[0] * grad_mixed[0] + window[1] * grad_mixed[1]
    wave_im = window[0] * grad_mixed[1] - window[1] * grad_mixed[0]
    return (jnp.stack([object_re, object_im]), jnp.stack([wave_re, wave_im]).astype(jnp.bfloat16))


def local(probe_wave, propagator, object_slices, positions, intensities):
    window_size = probe_wave.shape[1]
    band_rows = object_slices.shape[2]
    reach_bands = window_size // band_rows
    local_count = positions.shape[0]
    own_band = object_slices[:, 0]
    fetched = [passed_along(own_band, "scan", -distance) for distance in range(1, reach_bands + 1)]
    widened = jnp.concatenate([own_band] + fetched, axis=1)
    transform = dft_table(window_size)
    section_index = lax.axis_index("cuts")
    sections = lax.axis_size("cuts")
    turn_count = local_count + sections - 1
    is_final = section_index == sections - 1

    def corner_at(member):
        return (jnp.int32(0), positions[member, 0] % band_rows, positions[member, 1])

    def window_at(member):
        return lax.dynamic_slice(widened, corner_at(member), (2, window_size, window_size))

    zero_wave = jnp.zeros((2, window_size, window_size), jnp.bfloat16)
    zero_stack = jnp.zeros((local_count, 2, window_size, window_size), jnp.bfloat16)

    def forward_turn(turn_step, loop_state):
        received, section_inputs, exit_waves = loop_state
        member = turn_step - section_index
        active = (member >= 0) & (member < local_count)
        clamped = jnp.clip(member, 0, local_count - 1)
        wave_in = jnp.where(section_index == 0, probe_wave, received)
        wave_out = lax.cond(
            active,
            lambda: forward_section(wave_in, window_at(clamped), propagator),
            lambda: zero_wave,
        )
        section_inputs = section_inputs.at[clamped].set(
            jnp.where(active, wave_in, section_inputs[clamped])
        )
        exit_waves = exit_waves.at[clamped].set(jnp.where(active, wave_out, exit_waves[clamped]))
        received = shifted(wave_out, "cuts", 1)
        return (received, section_inputs, exit_waves)

    received, section_inputs, exit_waves = lax.fori_loop(
        0, turn_count, forward_turn, (zero_wave, zero_stack, zero_stack)
    )

    def all_residues():
        return lax.map(
            lambda paired: far_gradient(paired[0], paired[1], transform), (exit_waves, intensities)
        )

    residues = lax.cond(is_final, all_residues, lambda: zero_stack)
    zero_object = jnp.zeros((2, window_size, window_size), jnp.float32)
    initial_sum = jnp.zeros((2, (reach_bands + 1) * band_rows, widened.shape[2]), jnp.float32)

    def backward_turn(turn_step, loop_state):
        received, gradient_sum = loop_state
        member = turn_step - (sections - 1 - section_index)
        active = (member >= 0) & (member < local_count)
        clamped = jnp.clip(member, 0, local_count - 1)
        grad_in = jnp.where(is_final, residues[clamped], received)

        def active_branch():
            return adjoint_section(grad_in, section_inputs[clamped], window_at(clamped), propagator)

        def skipped_branch():
            return (zero_object, zero_wave)

        object_grad, wave_grad = lax.cond(active, active_branch, skipped_branch)
        corner = corner_at(clamped)
        current = lax.dynamic_slice(gradient_sum, corner, (2, window_size, window_size))
        gradient_sum = lax.dynamic_update_slice(gradient_sum, current + object_grad, corner)
        received = shifted(wave_grad, "cuts", -1)
        return (received, gradient_sum)

    received, gradient_sum = lax.fori_loop(0, turn_count, backward_turn, (zero_wave, initial_sum))
    pieces = [
        gradient_sum[:, number * band_rows : (number + 1) * band_rows]
        for number in range(reach_bands + 1)
    ]
    arrived = [
        passed_along(pieces[distance].astype(jnp.bfloat16), "scan", distance).astype(jnp.float32)
        for distance in range(1, reach_bands + 1)
    ]
    summed = pieces[0]
    for incoming in arrived:
        summed = summed + incoming
    return summed[:, None]


def solution(mesh):
    in_specs = (P(), P(), P(None, "cuts", "scan", None), P("scan", None), P("scan", None, None))
    out_specs = P(None, "cuts", "scan", None)
    return jax.shard_map(local, mesh=mesh, in_specs=in_specs, out_specs=out_specs, check_vma=False)
```

profile of v0, /device:TPU:1, one launch (start us, length us, event | category | flops | bytes accessed | tf_op | source)
XLA Modules:
  0.0 732.1 jit_solution(616547449890609695)
XLA Ops:
  4.3 5.0 collective-permute-start.3
  12.6 4.4 multiply_convert_fusion
  20.3 32.0 %collective-permute-done.2 = f32[2,128,2048]{1,2,0:T(8,128)} collective-permute-done((f32[2,128,2048]{1,2,0:T(8,128)}, f32[2,128,2048]{1,2,0:T(8,128)}, u32[]{:S(2)}, u32[]{:S(2)}) %collective-permute-start.2) | collective-permute-done | bytes 2097184 | tf_op jit(solution)/shard_map/ppermute | solution.py:11
  58.6 108.7 %collective-permute-done.4 = f32[2,128,2048]{1,2,0:T(8,128)} collective-permute-done((f32[2,128,2048]{1,2,0:T(8,128)}, f32[2,128,2048]{1,2,0:T(8,128)}, u32[]{:S(2)}, u32[]{:S(2)}) %collective-permute-start.4) | collective-permute-done | bytes 2097184 | tf_op jit(solution)/shard_map/ppermute | solution.py:11
  173.6 11.4 %copy.10 = f32[2,640,2048]{2,1,0:T(8,128)} copy(f32[2,640,2048]{1,2,0:T(8,128)} %constant_dynamic-update-slice_fusion.1) | data formatting | bytes 20971520 | tf_op jit(solution)/shard_map/while | solution.py:116
  189.0 189.9 %while.49 = (s32[]{:T(128)}, bf16[2,512,512]{2,1,0:T(8,128)(2,1)}, bf16[2,2,512,512]{2,3,1,0:T(8,128)(2,1)}, bf16[2,2,512,512]{3,2,1,0:T(8,128)(2,1)}, s32[]{:T(...) while((s32[]{:T(128)}, bf16[2,512,512]{2,1,0:T(8,128)(2,1)}, ...), condition=%wide.region_4.5_spmd, body=%wide.region_0.4_spmd.sunk | while | flops 2155347968 | bytes 65013376 | solution.py:116
  192.5 3.5 bitcast_select_fusion.6
  195.9 11.7 %conditional.6 = (bf16[2,512,512]{2,1,0:T(8,128)(2,1)}) conditional(s32[]{:T(128)} %convert_element_type.161, () %tuple.149, (bf16[2,512,512]{2,1,0:T(8,128)(2,1)S(1)}, s32[]{:T(128)}, s32[2,2]{1,0:T(2,128)S(1)}, f32[2,640,2048]{2,1,0:T(8,128)}, bf16[2,512,512]{2,1,0:T(8,128)(2,1)S(1)}) %tuple.150), branch_computations={%region_1.1_spmd, %region_2.2_spmd} | conditional | flops 2152726528 | bytes 25166088 | solution.py:104
  216.7 12.0 %collective-permute-done = bf16[2,512,512]{2,1,0:T(8,128)(2,1)} collective-permute-done((bf16[2,512,512]{2,1,0:T(8,128)(2,1)}, bf16[2,512,512]{2,1,0:T(8,128)(2,1)}, u32[]{:S(2)}, u32[]{:S(2)}) %collective-permute-start) | collective-permute-done | bytes 1048608 | tf_op jit(solution)/shard_map/while/body/eval_jaxpr/ppermute | solution.py:17
  232.2 3.5 bitcast_select_fusion.6
  235.6 11.7 %conditional.6 = (bf16[2,512,512]{2,1,0:T(8,128)(2,1)}) conditional(s32[]{:T(128)} %convert_element_type.161, () %tuple.149, (bf16[2,512,512]{2,1,0:T(8,128)(2,1)S(1)}, s32[]{:T(128)}, s32[2,2]{1,0:T(2,128)S(1)}, f32[2,640,2048]{2,1,0:T(8,128)}, bf16[2,512,512]{2,1,0:T(8,128)(2,1)S(1)}) %tuple.150), branch_computations={%region_1.1_spmd, %region_2.2_spmd} | conditional | flops 2152726528 | bytes 25166088 | solution.py:104
  247.3 5.1 collective-permute-start
  259.1 11.3 %collective-permute-done = bf16[2,512,512]{2,1,0:T(8,128)(2,1)} collective-permute-done((bf16[2,512,512]{2,1,0:T(8,128)(2,1)}, bf16[2,512,512]{2,1,0:T(8,128)(2,1)}, u32[]{:S(2)}, u32[]{:S(2)}) %collective-permute-start) | collective-permute-done | bytes 1048608 | tf_op jit(solution)/shard_map/while/body/eval_jaxpr/ppermute | solution.py:17
  273.9 3.5 bitcast_select_fusion.6
  278.4 15.6 %collective-permute-start = (bf16[2,512,512]{2,1,0:T(8,128)(2,1)}, bf16[2,512,512]{2,1,0:T(8,128)(2,1)}, u32[]{:S(2)}, u32[]{:S(2)}) collective-permute-start(bf16[2,512,512]{2,1,0:T(8,128)(2,1)} %get-tuple-element.1074), channel_id=1, source_target_pairs={{0,1},{1,2},{2,3},{4,5},{5,6},{6,7},{8,9},{9,10},{10,11},{12,13},{... | collective-permute-start | bytes 3145736 | tf_op jit(solution)/shard_map/while/body/eval_jaxpr/ppermute | solution.py:17
  299.6 11.6 %collective-permute-done = bf16[2,512,512]{2,1,0:T(8,128)(2,1)} collective-permute-done((bf16[2,512,512]{2,1,0:T(8,128)(2,1)}, bf16[2,512,512]{2,1,0:T(8,128)(2,1)}, u32[]{:S(2)}, u32[]{:S(2)}) %collective-permute-start) | collective-permute-done | bytes 1048608 | tf_op jit(solution)/shard_map/while/body/eval_jaxpr/ppermute | solution.py:17
  314.7 3.5 bitcast_select_fusion.6
  319.2 5.1 collective-permute-start
  329.8 10.7 %collective-permute-done = bf16[2,512,512]{2,1,0:T(8,128)(2,1)} collective-permute-done((bf16[2,512,512]{2,1,0:T(8,128)(2,1)}, bf16[2,512,512]{2,1,0:T(8,128)(2,1)}, u32[]{:S(2)}, u32[]{:S(2)}) %collective-permute-start) | collective-permute-done | bytes 1048608 | tf_op jit(solution)/shard_map/while/body/eval_jaxpr/ppermute | solution.py:17
  344.0 3.5 bitcast_select_fusion.6
  348.5 14.7 %collective-permute-start = (bf16[2,512,512]{2,1,0:T(8,128)(2,1)}, bf16[2,512,512]{2,1,0:T(8,128)(2,1)}, u32[]{:S(2)}, u32[]{:S(2)}) collective-permute-start(bf16[2,512,512]{2,1,0:T(8,128)(2,1)} %get-tuple-element.1074), channel_id=1, source_target_pairs={{0,1},{1,2},{2,3},{4,5},{5,6},{6,7},{8,9},{9,10},{10,11},{12,13},{... | collective-permute-start | bytes 3145736 | tf_op jit(solution)/shard_map/while/body/eval_jaxpr/ppermute | solution.py:17
  368.7 10.2 %collective-permute-done = bf16[2,512,512]{2,1,0:T(8,128)(2,1)} collective-permute-done((bf16[2,512,512]{2,1,0:T(8,128)(2,1)}, bf16[2,512,512]{2,1,0:T(8,128)(2,1)}, u32[]{:S(2)}, u32[]{:S(2)}) %collective-permute-start) | collective-permute-done | bytes 1048608 | tf_op jit(solution)/shard_map/while/body/eval_jaxpr/ppermute | solution.py:17
  381.6 5.3 broadcast_in_dim.28.clone
  386.9 251.2 %while.50 = (s32[]{:T(128)}, bf16[2,512,512]{1,2,0:T(8,128)(2,1)}, f32[2,640,2048]{2,1,0:T(8,128)}, s32[]{:T(128)}, bf16[2,2,512,512]{2,3,1,0:T(8,128)(2,1)}, /*...) while((s32[]{:T(128)}, bf16[2,512,512]{1,2,0:T(8,128)(2,1)}, ...), condition=%wide.region_12.13_spmd, body=%wide.region_9.12_spmd.sunk | while | flops 2156396544 | bytes 73401136 | solution.py:149
  393.8 3.8 constant_dynamic-slice_fusion.16
  400.6 3.5 add.327
  406.0 14.4 %dynamic_update_slice.19 = f32[2,640,2048]{2,1,0:T(8,128)} dynamic-update-slice(f32[2,640,2048]{2,1,0:T(8,128)} %get-tuple-element.1041, f32[2,512,512]{2,1,0:T(8,128)S(1)} %copy.27, s32[]{:T(128)} %constant.302.clone.1..sunk.1, s32[]{:T(128)S(6)} %select_n.210, s32[]{:T(128)S(6)} %select_n.211) | dynamic-update-slice | bytes 4194308 | tf_op jit(solution)/shard_map/while/body/eval_jaxpr/dynamic_update_slice | solution.py:145
  427.3 3.8 constant_dynamic-slice_fusion.16
  434.0 3.5 add.327
  439.4 14.4 %dynamic_update_slice.19 = f32[2,640,2048]{2,1,0:T(8,128)} dynamic-update-slice(f32[2,640,2048]{2,1,0:T(8,128)} %get-tuple-element.1041, f32[2,512,512]{2,1,0:T(8,128)S(1)} %copy.27, s32[]{:T(128)} %constant.302.clone.1..sunk.1, s32[]{:T(128)S(6)} %select_n.210, s32[]{:T(128)S(6)} %select_n.211) | dynamic-update-slice | bytes 4194308 | tf_op jit(solution)/shard_map/while/body/eval_jaxpr/dynamic_update_slice | solution.py:145
  460.7 3.8 constant_dynamic-slice_fusion.16
  467.5 3.5 add.327
  472.8 14.4 %dynamic_update_slice.19 = f32[2,640,2048]{2,1,0:T(8,128)} dynamic-update-slice(f32[2,640,2048]{2,1,0:T(8,128)} %get-tuple-element.1041, f32[2,512,512]{2,1,0:T(8,128)S(1)} %copy.27, s32[]{:T(128)} %constant.302.clone.1..sunk.1, s32[]{:T(128)S(6)} %select_n.210, s32[]{:T(128)S(6)} %select_n.211) | dynamic-update-slice | bytes 4194308 | tf_op jit(solution)/shard_map/while/body/eval_jaxpr/dynamic_update_slice | solution.py:145
  487.2 45.3 %collective-permute-done.1 = bf16[2,512,512]{1,2,0:T(8,128)(2,1)} collective-permute-done((bf16[2,512,512]{1,2,0:T(8,128)(2,1)}, bf16[2,512,512]{1,2,0:T(8,128)(2,1)}, u32[]{:S(2)}, u32[]{:S(2)}) %collective-permute-start.1) | collective-permute-done | bytes 1048608 | tf_op jit(solution)/shard_map/while/body/eval_jaxpr/ppermute | solution.py:17
  532.5 15.5 %conditional.7 = (f32[2,512,512]{1,2,0:T(8,128)S(1)}, bf16[2,512,512]{1,2,0:T(8,128)(2,1)}) conditional(s32[]{:T(128)} %convert_element_type.162, () %tuple.153, (s32[]{:T(128)}, bf16[2,2,512,512]{2,3,1,0:T(8,128)(2,1)}, pred[]{:T(512)}, bf16[2,2,512,512]{3,2,1,0:T(8,128)(2,1)}, bf16[2,512,512]{1,2,0:T(8,128)(2,1)}, ...), branch_computations={%region_10.10_spmd, %region_11.11_spmd} | conditional | flops 2155872256 | bytes 46137640 | solution.py:142
  553.7 3.8 constant_dynamic-slice_fusion.16
  560.4 3.5 add.327
  565.8 14.4 %dynamic_update_slice.19 = f32[2,640,2048]{2,1,0:T(8,128)} dynamic-update-slice(f32[2,640,2048]{2,1,0:T(8,128)} %get-tuple-element.1041, f32[2,512,512]{2,1,0:T(8,128)S(1)} %copy.27, s32[]{:T(128)} %constant.302.clone.1..sunk.1, s32[]{:T(128)S(6)} %select_n.210, s32[]{:T(128)S(6)} %select_n.211) | dynamic-update-slice | bytes 4194308 | tf_op jit(solution)/shard_map/while/body/eval_jaxpr/dynamic_update_slice | solution.py:145
  580.2 10.7 %collective-permute-done.1 = bf16[2,512,512]{1,2,0:T(8,128)(2,1)} collective-permute-done((bf16[2,512,512]{1,2,0:T(8,128)(2,1)}, bf16[2,512,512]{1,2,0:T(8,128)(2,1)}, u32[]{:S(2)}, u32[]{:S(2)}) %collective-permute-start.1) | collective-permute-done | bytes 1048608 | tf_op jit(solution)/shard_map/while/body/eval_jaxpr/ppermute | solution.py:17
  590.8 15.5 %conditional.7 = (f32[2,512,512]{1,2,0:T(8,128)S(1)}, bf16[2,512,512]{1,2,0:T(8,128)(2,1)}) conditional(s32[]{:T(128)} %convert_element_type.162, () %tuple.153, (s32[]{:T(128)}, bf16[2,2,512,512]{2,3,1,0:T(8,128)(2,1)}, pred[]{:T(512)}, bf16[2,2,512,512]{3,2,1,0:T(8,128)(2,1)}, bf16[2,512,512]{1,2,0:T(8,128)(2,1)}, ...), branch_computations={%region_10.10_spmd, %region_11.11_spmd} | conditional | flops 2155872256 | bytes 46137640 | solution.py:142
  612.0 3.8 constant_dynamic-slice_fusion.16
  624.1 13.9 %dynamic_update_slice.19 = f32[2,640,2048]{2,1,0:T(8,128)} dynamic-update-slice(f32[2,640,2048]{2,1,0:T(8,128)} %get-tuple-element.1041, f32[2,512,512]{2,1,0:T(8,128)S(1)} %copy.27, s32[]{:T(128)} %constant.302.clone.1..sunk.1, s32[]{:T(128)S(6)} %select_n.210, s32[]{:T(128)S(6)} %select_n.211) | dynamic-update-slice | bytes 4194308 | tf_op jit(solution)/shard_map/while/body/eval_jaxpr/dynamic_update_slice | solution.py:145
  638.1 4.8 convert.76
  643.5 18.4 %collective-permute-done.6 = bf16[2,128,2048]{2,1,0:T(8,128)(2,1)S(1)} collective-permute-done((bf16[2,128,2048]{2,1,0:T(8,128)(2,1)S(1)}, bf16[2,128,2048]{2,1,0:T(8,128)(2,1)S(1)}, u32[]{:S(2)}, u32[]{:S(2)}) %collective-permute-start.6) | collective-permute-done | bytes 1048608 | tf_op jit(solution)/shard_map/ppermute | solution.py:11
  661.9 26.3 %collective-permute-done.9 = bf16[2,128,2048]{2,1,0:T(8,128)(2,1)S(1)} collective-permute-done((bf16[2,128,2048]{2,1,0:T(8,128)(2,1)S(1)}, bf16[2,128,2048]{2,1,0:T(8,128)(2,1)S(1)}, u32[]{:S(2)}, u32[]{:S(2)}) %collective-permute-start.9) | collective-permute-done | bytes 1048608 | tf_op jit(solution)/shard_map/ppermute | solution.py:11
  688.2 18.6 %collective-permute-done.8 = bf16[2,128,2048]{2,1,0:T(8,128)(2,1)S(1)} collective-permute-done((bf16[2,128,2048]{2,1,0:T(8,128)(2,1)S(1)}, bf16[2,128,2048]{2,1,0:T(8,128)(2,1)S(1)}, u32[]{:S(2)}, u32[]{:S(2)}) %collective-permute-start.8) | collective-permute-done | bytes 1048608 | tf_op jit(solution)/shard_map/ppermute | solution.py:11
  706.9 21.5 %collective-permute-done.7 = bf16[2,128,2048]{2,1,0:T(8,128)(2,1)S(1)} collective-permute-done((bf16[2,128,2048]{2,1,0:T(8,128)(2,1)S(1)}, bf16[2,128,2048]{2,1,0:T(8,128)(2,1)S(1)}, u32[]{:S(2)}, u32[]{:S(2)}) %collective-permute-start.7) | collective-permute-done | bytes 1048608 | tf_op jit(solution)/shard_map/ppermute | solution.py:11
  728.4 3.7 add_bitcast_fusion
  (176 shorter events, 172.9 us)
Async XLA Ops:
  2.9 49.4 %collective-permute-start.2 = (f32[2,128,2048]{1,2,0:T(8,128)}, f32[2,128,2048]{1,2,0:T(8,128)}, u32[]{:S(2)}, u32[]{:S(2)}) collective-permute-start(f32[2,128,2048]{1,2,0:T(8,128)} %bitcast.46), channel_id=1, source_target_pairs={{0,124},{4,0},{8,4},{12,8},{16,12},{20,16},{24,20},{28,24},{32,28}... | collective-permute-start | bytes 6291464 | tf_op jit(solution)/shard_map/ppermute | solution.py:11
  4.3 51.2 %collective-permute-start.3 = (f32[2,128,2048]{1,2,0:T(8,128)}, f32[2,128,2048]{1,2,0:T(8,128)}, u32[]{:S(2)}, u32[]{:S(2)}) collective-permute-start(f32[2,128,2048]{1,2,0:T(8,128)} %bitcast.46), channel_id=1, source_target_pairs={{0,120},{4,124},{8,0},{12,4},{16,8},{20,12},{24,16},{28,20},{32,24... | collective-permute-start | bytes 6291464 | tf_op jit(solution)/shard_map/ppermute | solution.py:11
  9.3 158.0 %collective-permute-start.4 = (f32[2,128,2048]{1,2,0:T(8,128)}, f32[2,128,2048]{1,2,0:T(8,128)}, u32[]{:S(2)}, u32[]{:S(2)}) collective-permute-start(f32[2,128,2048]{1,2,0:T(8,128)} %bitcast.46), channel_id=1, source_target_pairs={{0,116},{4,120},{8,124},{12,0},{16,4},{20,8},{24,12},{28,16},{32,2... | collective-permute-start | bytes 6291464 | tf_op jit(solution)/shard_map/ppermute | solution.py:11
  10.0 160.4 %collective-permute-start.5 = (f32[2,128,2048]{1,2,0:T(8,128)}, f32[2,128,2048]{1,2,0:T(8,128)}, u32[]{:S(2)}, u32[]{:S(2)}) collective-permute-start(f32[2,128,2048]{1,2,0:T(8,128)} %bitcast.46), channel_id=1, source_target_pairs={{0,112},{4,116},{8,120},{12,124},{16,0},{20,4},{24,8},{28,12},{32,... | collective-permute-start | bytes 6291464 | tf_op jit(solution)/shard_map/ppermute | solution.py:11
  186.0 3.0 copy-start
  186.0 3.0 copy-start.5
  186.0 3.0 copy-start.6
  207.6 21.1 %collective-permute-start = (bf16[2,512,512]{2,1,0:T(8,128)(2,1)}, bf16[2,512,512]{2,1,0:T(8,128)(2,1)}, u32[]{:S(2)}, u32[]{:S(2)}) collective-permute-start(bf16[2,512,512]{2,1,0:T(8,128)(2,1)} %get-tuple-element.1074), channel_id=1, source_target_pairs={{0,1},{1,2},{2,3},{4,5},{5,6},{6,7},{8,9},{9,10},{10,11},{12,13},{... | collective-permute-start | bytes 3145736 | tf_op jit(solution)/shard_map/while/body/eval_jaxpr/ppermute | solution.py:17
  211.4 1.9 copy-start.1
  213.4 15.3 %copy-start.2 = (bf16[2,2,512,512]{2,3,1,0:T(8,128)(2,1)}, bf16[2,2,512,512]{2,3,1,0:T(8,128)(2,1)S(1)}, u32[]{:S(2)}) copy-start(bf16[2,2,512,512]{2,3,1,0:T(8,128)(2,1)S(1)} %constant_dynamic-update-slice_fusion.7) | copy-start | bytes 6291460 | tf_op jit(solution)/shard_map/while
  247.3 23.1 %collective-permute-start = (bf16[2,512,512]{2,1,0:T(8,128)(2,1)}, bf16[2,512,512]{2,1,0:T(8,128)(2,1)}, u32[]{:S(2)}, u32[]{:S(2)}) collective-permute-start(bf16[2,512,512]{2,1,0:T(8,128)(2,1)} %get-tuple-element.1074), channel_id=1, source_target_pairs={{0,1},{1,2},{2,3},{4,5},{5,6},{6,7},{8,9},{9,10},{10,11},{12,13},{... | collective-permute-start | bytes 3145736 | tf_op jit(solution)/shard_map/while/body/eval_jaxpr/ppermute | solution.py:17
  253.9 1.9 copy-start.1
  255.9 14.6 %copy-start.2 = (bf16[2,2,512,512]{2,3,1,0:T(8,128)(2,1)}, bf16[2,2,512,512]{2,3,1,0:T(8,128)(2,1)S(1)}, u32[]{:S(2)}) copy-start(bf16[2,2,512,512]{2,3,1,0:T(8,128)(2,1)S(1)} %constant_dynamic-update-slice_fusion.7) | copy-start | bytes 6291460 | tf_op jit(solution)/shard_map/while
  278.4 32.8 %collective-permute-start = (bf16[2,512,512]{2,1,0:T(8,128)(2,1)}, bf16[2,512,512]{2,1,0:T(8,128)(2,1)}, u32[]{:S(2)}, u32[]{:S(2)}) collective-permute-start(bf16[2,512,512]{2,1,0:T(8,128)(2,1)} %get-tuple-element.1074), channel_id=1, source_target_pairs={{0,1},{1,2},{2,3},{4,5},{5,6},{6,7},{8,9},{9,10},{10,11},{12,13},{... | collective-permute-start | bytes 3145736 | tf_op jit(solution)/shard_map/while/body/eval_jaxpr/ppermute | solution.py:17
  295.6 1.9 copy-start.1
  297.6 13.6 %copy-start.2 = (bf16[2,2,512,512]{2,3,1,0:T(8,128)(2,1)}, bf16[2,2,512,512]{2,3,1,0:T(8,128)(2,1)S(1)}, u32[]{:S(2)}) copy-start(bf16[2,2,512,512]{2,3,1,0:T(8,128)(2,1)S(1)} %constant_dynamic-update-slice_fusion.7) | copy-start | bytes 6291460 | tf_op jit(solution)/shard_map/while
  319.2 21.3 %collective-permute-start = (bf16[2,512,512]{2,1,0:T(8,128)(2,1)}, bf16[2,512,512]{2,1,0:T(8,128)(2,1)}, u32[]{:S(2)}, u32[]{:S(2)}) collective-permute-start(bf16[2,512,512]{2,1,0:T(8,128)(2,1)} %get-tuple-element.1074), channel_id=1, source_target_pairs={{0,1},{1,2},{2,3},{4,5},{5,6},{6,7},{8,9},{9,10},{10,11},{12,13},{... | collective-permute-start | bytes 3145736 | tf_op jit(solution)/shard_map/while/body/eval_jaxpr/ppermute | solution.py:17
  325.8 1.9 copy-start.1
  327.8 12.7 %copy-start.2 = (bf16[2,2,512,512]{2,3,1,0:T(8,128)(2,1)}, bf16[2,2,512,512]{2,3,1,0:T(8,128)(2,1)S(1)}, u32[]{:S(2)}) copy-start(bf16[2,2,512,512]{2,3,1,0:T(8,128)(2,1)S(1)} %constant_dynamic-update-slice_fusion.7) | copy-start | bytes 6291460 | tf_op jit(solution)/shard_map/while
  348.5 30.4 %collective-permute-start = (bf16[2,512,512]{2,1,0:T(8,128)(2,1)}, bf16[2,512,512]{2,1,0:T(8,128)(2,1)}, u32[]{:S(2)}, u32[]{:S(2)}) collective-permute-start(bf16[2,512,512]{2,1,0:T(8,128)(2,1)} %get-tuple-element.1074), channel_id=1, source_target_pairs={{0,1},{1,2},{2,3},{4,5},{5,6},{6,7},{8,9},{9,10},{10,11},{12,13},{... | collective-permute-start | bytes 3145736 | tf_op jit(solution)/shard_map/while/body/eval_jaxpr/ppermute | solution.py:17
  364.7 1.9 copy-start.1
  366.7 12.3 %copy-start.2 = (bf16[2,2,512,512]{2,3,1,0:T(8,128)(2,1)}, bf16[2,2,512,512]{2,3,1,0:T(8,128)(2,1)S(1)}, u32[]{:S(2)}) copy-start(bf16[2,2,512,512]{2,3,1,0:T(8,128)(2,1)S(1)} %constant_dynamic-update-slice_fusion.7) | copy-start | bytes 6291460 | tf_op jit(solution)/shard_map/while
  388.2 32.1 %collective-permute-start.1 = (bf16[2,512,512]{1,2,0:T(8,128)(2,1)}, bf16[2,512,512]{1,2,0:T(8,128)(2,1)}, u32[]{:S(2)}, u32[]{:S(2)}) collective-permute-start(bf16[2,512,512]{1,2,0:T(8,128)(2,1)} %get-tuple-element.934), channel_id=1, source_target_pairs={{1,0},{2,1},{3,2},{5,4},{6,5},{7,6},{9,8},{10,9},{11,10},{13,12},{... | collective-permute-start | bytes 3145736 | tf_op jit(solution)/shard_map/while/body/eval_jaxpr/ppermute | solution.py:17
  421.7 32.1 %collective-permute-start.1 = (bf16[2,512,512]{1,2,0:T(8,128)(2,1)}, bf16[2,512,512]{1,2,0:T(8,128)(2,1)}, u32[]{:S(2)}, u32[]{:S(2)}) collective-permute-start(bf16[2,512,512]{1,2,0:T(8,128)(2,1)} %get-tuple-element.934), channel_id=1, source_target_pairs={{1,0},{2,1},{3,2},{5,4},{6,5},{7,6},{9,8},{10,9},{11,10},{13,12},{... | collective-permute-start | bytes 3145736 | tf_op jit(solution)/shard_map/while/body/eval_jaxpr/ppermute | solution.py:17
  455.1 77.4 %collective-permute-start.1 = (bf16[2,512,512]{1,2,0:T(8,128)(2,1)}, bf16[2,512,512]{1,2,0:T(8,128)(2,1)}, u32[]{:S(2)}, u32[]{:S(2)}) collective-permute-start(bf16[2,512,512]{1,2,0:T(8,128)(2,1)} %get-tuple-element.934), channel_id=1, source_target_pairs={{1,0},{2,1},{3,2},{5,4},{6,5},{7,6},{9,8},{10,9},{11,10},{13,12},{... | collective-permute-start | bytes 3145736 | tf_op jit(solution)/shard_map/while/body/eval_jaxpr/ppermute | solution.py:17
  542.2 1.6 copy-start.3
  548.1 42.8 %collective-permute-start.1 = (bf16[2,512,512]{1,2,0:T(8,128)(2,1)}, bf16[2,512,512]{1,2,0:T(8,128)(2,1)}, u32[]{:S(2)}, u32[]{:S(2)}) collective-permute-start(bf16[2,512,512]{1,2,0:T(8,128)(2,1)} %get-tuple-element.934), channel_id=1, source_target_pairs={{1,0},{2,1},{3,2},{5,4},{6,5},{7,6},{9,8},{10,9},{11,10},{13,12},{... | collective-permute-start | bytes 3145736 | tf_op jit(solution)/shard_map/while/body/eval_jaxpr/ppermute | solution.py:17
  600.5 1.6 copy-start.3
  606.4 31.7 %collective-permute-start.1 = (bf16[2,512,512]{1,2,0:T(8,128)(2,1)}, bf16[2,512,512]{1,2,0:T(8,128)(2,1)}, u32[]{:S(2)}, u32[]{:S(2)}) collective-permute-start(bf16[2,512,512]{1,2,0:T(8,128)(2,1)} %get-tuple-element.934), channel_id=1, source_target_pairs={{1,0},{2,1},{3,2},{5,4},{6,5},{7,6},{9,8},{10,9},{11,10},{13,12},{... | collective-permute-start | bytes 3145736 | tf_op jit(solution)/shard_map/while/body/eval_jaxpr/ppermute | solution.py:17
  643.2 18.7 %collective-permute-start.6 = (bf16[2,128,2048]{2,1,0:T(8,128)(2,1)S(1)}, bf16[2,128,2048]{2,1,0:T(8,128)(2,1)S(1)}, u32[]{:S(2)}, u32[]{:S(2)}) collective-permute-start(bf16[2,128,2048]{2,1,0:T(8,128)(2,1)S(1)} %get-tuple-element.765), channel_id=1, source_target_pairs={{0,4},{4,8},{8,12},{12,16},{16,20},{20,24},{24,28},{28,32},{32,36}... | collective-permute-start | bytes 3145736 | tf_op jit(solution)/shard_map/ppermute | solution.py:11
  643.3 44.9 %collective-permute-start.9 = (bf16[2,128,2048]{2,1,0:T(8,128)(2,1)S(1)}, bf16[2,128,2048]{2,1,0:T(8,128)(2,1)S(1)}, u32[]{:S(2)}, u32[]{:S(2)}) collective-permute-start(bf16[2,128,2048]{2,1,0:T(8,128)(2,1)S(1)} %get-tuple-element.766), channel_id=1, source_target_pairs={{0,16},{4,20},{8,24},{12,28},{16,32},{20,36},{24,40},{28,44},{32,4... | collective-permute-start | bytes 3145736 | tf_op jit(solution)/shard_map/ppermute | solution.py:11
  643.4 63.5 %collective-permute-start.8 = (bf16[2,128,2048]{2,1,0:T(8,128)(2,1)S(1)}, bf16[2,128,2048]{2,1,0:T(8,128)(2,1)S(1)}, u32[]{:S(2)}, u32[]{:S(2)}) collective-permute-start(bf16[2,128,2048]{2,1,0:T(8,128)(2,1)S(1)} %get-tuple-element.767), channel_id=1, source_target_pairs={{0,12},{4,16},{8,20},{12,24},{16,28},{20,32},{24,36},{28,40},{32,4... | collective-permute-start | bytes 3145736 | tf_op jit(solution)/shard_map/ppermute | solution.py:11
  643.4 84.9 %collective-permute-start.7 = (bf16[2,128,2048]{2,1,0:T(8,128)(2,1)S(1)}, bf16[2,128,2048]{2,1,0:T(8,128)(2,1)S(1)}, u32[]{:S(2)}, u32[]{:S(2)}) collective-permute-start(bf16[2,128,2048]{2,1,0:T(8,128)(2,1)S(1)} %get-tuple-element.768), channel_id=1, source_target_pairs={{0,8},{4,12},{8,16},{12,20},{16,24},{20,28},{24,32},{28,36},{32,40... | collective-permute-start | bytes 3145736 | tf_op jit(solution)/shard_map/ppermute | solution.py:11
where the time goes:
time: 738 us; the launch traced here: 732 us
  waiting for transfers between devices  338 us (46%)
  local copies, waits for them, and re-layouts  205 us (28%)
  other arithmetic  76.2 us (10%)
  starting transfers between devices  59.2 us (8%)
  loops' own time  34.1 us (5%)
  matrix products  20.2 us (3%)
    ppermute x8, waiting for transfers between devices, passed_along(): lax.ppermute(shard, axis, [(i, (i + by) % devices) for i in range(devices)])  226 us
    ppermute x10, waiting for transfers between devices, shifted(): return lax.ppermute(block, axis, route)  112 us
    dynamic_update_slice x10, local copies, waits for them, and re-layouts, backward_turn(): lax.dynamic_update_slice(gradient_sum, current + object_grad, corner)  81 us
    ppermute x10, starting transfers between devices, shifted(): return lax.ppermute(block, axis, route)  49.1 us
    dynamic_slice x10, local copies, waits for them, and re-layouts, backward_turn(): lax.dynamic_slice(gradient_sum, corner, (2, window_size, window_size))  33.7 us
    another operation x12, other arithmetic  30.3 us
    another operation x1, loops' own time, local(): lax.fori_loop(0, turn_count, backward_turn, (zero_wave, initial_sum))  18.7 us
    add x5, other arithmetic, backward_turn(): current + object_grad  17.3 us
  transfers between devices with their start and end apart: 18, of which 13 were waited for; matrix products, arithmetic and copies ran while one was open for 25% of the time, Pallas kernels for 0%

commit v1 on v0

v1 whole, which is shorter than its diff:
```python
import functools
import math

import jax
import jax.numpy as jnp
import numpy as np
from jax import lax
from jax.experimental import pallas as pl
from jax.experimental.pallas import tpu as pltpu
from jax.sharding import PartitionSpec as P

MESH = pl.DeviceIdType.MESH
BF16 = jnp.bfloat16
F32 = jnp.float32
REACH = 5
LANES = 128


def dft_table(length):
    serial = np.arange(length, dtype=np.int32)
    angle_index = serial[:, None] * serial[None, :] % length
    angle = angle_index.astype(np.float32) * np.float32(2.0 * math.pi / length)
    scale = np.float32(1.0 / math.sqrt(length))
    return jnp.asarray(
        np.stack([np.cos(angle) * scale, -np.sin(angle) * scale]), dtype=BF16
    )


def place():
    me = lax.axis_index("scan")
    cut = lax.axis_index("cuts")
    return me, cut, lax.rem(me, 2)


def wrapped(index, count):
    return lax.rem(index + 2 * count, count)


def worker(me, d, m, count):
    band = wrapped(me - d, count)
    return wrapped(me - d + 2, count), 2 * lax.rem(band, 2) + m


def column_split(column, width, window):
    base = jnp.minimum(column // LANES * LANES, width - window - LANES)
    return pl.multiple_of(base, LANES), column - base


def positions_kernel(count, pos_ref, pos_out, tile, pos_in, psend, precv):
    me, cut, parity = place()
    barrier = pltpu.get_barrier_semaphore()
    for d in range(1, REACH):
        pl.semaphore_signal(barrier, inc=1, device_id=(wrapped(me - d, count), cut), device_id_type=MESH)
    lane = lax.broadcasted_iota(jnp.int32, (8, LANES), 1)
    values = jnp.zeros((8, LANES), jnp.int32)
    for n in range(4):
        values = jnp.where(lane == n, pos_ref[n // 2, n % 2], values)
    tile[...] = values
    pos_out[0] = values
    pl.semaphore_wait(barrier, REACH - 1)
    copies = []
    for d in range(1, REACH):
        copy = pltpu.make_async_remote_copy(
            src_ref=tile, dst_ref=pos_in.at[d - 1], send_sem=psend.at[d - 1], recv_sem=precv.at[d - 1],
            device_id=(wrapped(me + d, count), cut), device_id_type=MESH)
        copy.start()
        copies.append(copy)
    for d in range(1, REACH):
        copies[d - 1].wait()
        pos_out[d] = pos_in[d - 1]


def pack_kernel(pos_ref, band, stage, band2):
    window = stage.shape[3]
    width = band.shape[3]
    band2[:, :128] = band[:, 0]
    band2[:, 128:] = band[:, 0]
    lane5 = lax.broadcasted_iota(jnp.int32, (5, 8, LANES), 2)
    sub4 = lax.broadcasted_iota(jnp.int32, (4, 8, LANES), 1)
    def pack(slot, row, column):
        offset = lax.rem(row, 128)
        tile_row, low_row = offset // 8, lax.rem(offset, 8)
        base, shift = column_split(column, width, window)
        turn = lax.rem(LANES - shift, LANES)
        lift = lax.rem(8 - low_row, 8)
        keep = lane5 + shift < LANES
        keep_row = sub4 + low_row < 8

        for part in range(2):
            def strip(q, carry):
                rows = pl.ds(pl.multiple_of(tile_row * 8 + q * 32, 8), 40)
                block = band2[part, rows, pl.ds(base, window + LANES)]
                turned = [
                    pltpu.roll(block[:, j * LANES:(j + 1) * LANES].reshape(5, 8, LANES), turn, 2)
                    for j in range(window // LANES + 1)
                ]
                for j in range(window // LANES):
                    lifted = pltpu.roll(jnp.where(keep, turned[j], turned[j + 1]), lift, 1)
                    made = jnp.where(keep_row, lifted[:4], lifted[1:]).reshape(32, LANES)
                    stage[slot, part, pl.ds(pl.multiple_of(q * 32, 32), 32), j * LANES:(j + 1) * LANES] = made.astype(BF16)
                return carry
            lax.fori_loop(0, 4, strip, 0)

    for d in range(REACH):
        for m in range(2):
            pack(d * 2 + m, pos_ref[d, 0, 2 * m], pos_ref[d, 0, 2 * m + 1])


def send_kernel(count, stage, int_ref, win_ref, own_int_ref, win_send, win_recv, self_sem, isend, irecv):
    me, cut, parity = place()
    active = (cut // 2) == parity
    barrier = pltpu.get_barrier_semaphore()

    @pl.when(active)
    def _():
        pl.semaphore_signal(barrier, inc=1, device_id=(wrapped(me - 2, count), cut), device_id_type=MESH)
        for d in range(REACH):
            for k in range(4):
                def greet():
                    pl.semaphore_signal(
                        barrier, inc=1, device_id=(wrapped(me - 2 + d, count), jnp.int32(k)), device_id_type=MESH
                    )
                if d == 2:
                    pl.when(cut != k)(greet)
                else:
                    greet()

    pl.semaphore_wait(barrier, 10)

    icopy = pltpu.make_async_remote_copy(
        src_ref=int_ref.at[lax.rem(cut, 2)], dst_ref=own_int_ref, send_sem=isend, recv_sem=irecv,
        device_id=(wrapped(me + 2, count), cut), device_id_type=MESH)

    def window_copy(d, m):
        slot = d * 2 + m
        scan_to, cut_to = worker(me, d, m, count)
        return pltpu.make_async_remote_copy(
            src_ref=stage.at[slot], dst_ref=win_ref.at[cut, :, pl.ds(d * 128, 128), :],
            send_sem=win_send.at[slot], recv_sem=win_recv.at[cut, d],
            device_id=(scan_to, cut_to), device_id_type=MESH)

    def local_copy(slot):
        return pltpu.make_async_copy(stage.at[slot], win_ref.at[cut, :, pl.ds(256, 128), :], self_sem)

    def send(d, m):
        if d == 2:
            mine = cut == 2 * parity + m
            pl.when(jnp.logical_not(mine))(lambda: window_copy(d, m).start())
            pl.when(mine)(lambda: local_copy(d * 2 + m).start())
        else:
            window_copy(d, m).start()

    for d in range(REACH):
        for m in range(2):
            send(d, m)
    @pl.when(active)
    def _():
        icopy.start()
    for d in range(REACH):
        for m in range(2):
            if d == 2:
                mine = cut == 2 * parity + m
                pl.when(jnp.logical_not(mine))(lambda: window_copy(d, m).wait_send())
                pl.when(mine)(lambda: local_copy(d * 2 + m).wait())
            else:
                window_copy(d, m).wait_send()

    @pl.when(active)
    def _():
        for d in range(REACH):
            for k in range(4):
                def arrive():
                    pltpu.make_async_copy(
                        stage.at[0], win_ref.at[k, :, pl.ds(d * 128, 128), :], win_recv.at[k, d]).wait()
                if d == 2:
                    pl.when(cut != k)(arrive)
                else:
                    arrive()
        icopy.wait()


def chain_kernel(pos_ref, win, probe, prop, table, intensity, out,
                 big_m, big_mt, big_f, big_ft, upright, flat, waves, far):
    me, cut, parity = place()
    size = probe.shape[1]
    slices = win.shape[0]
    active = (cut // 2) == parity

    def dot(a, b):
        return jnp.dot(a, b, preferred_element_type=F32)

    def left(big):
        def step(n, carry):
            cols = pl.ds(pl.multiple_of(n * 256, 256), 256)
            cols_im = pl.ds(pl.multiple_of(size + n * 256, 256), 256)
            got = dot(big[...], upright[:, cols])
            flat[:, cols] = got[:size].astype(BF16)
            flat[:, cols_im] = got[size:].astype(BF16)
            return carry
        lax.fori_loop(0, size // 256, step, 0)

    def right(big, put):
        def step(n, carry):
            cols = pl.ds(pl.multiple_of(n * 256, 256), 256)
            cols_im = pl.ds(pl.multiple_of(size + n * 256, 256), 256)
            put(cols, dot(flat[...], big[:, cols]), dot(flat[...], big[:, cols_im]))
            return carry
        lax.fori_loop(0, size // 256, step, 0)

    @pl.when(active)
    def _():
        offset = lax.rem(pos_ref[2, 0, 2 * lax.rem(cut, 2)], 128)
        for big, big_t, src in ((big_m, big_mt, prop), (big_f, big_ft, table)):
            re, im = src[0], src[1]
            re_t, im_t = re.T, im.T
            big[:size, :size] = re
            big[:size, size:] = -im
            big[size:, :size] = im
            big[size:, size:] = re
            big_t[:size, :size] = re_t
            big_t[:size, size:] = im_t
            big_t[size:, :size] = -im_t
            big_t[size:, size:] = re_t
        waves[0] = probe[...]

        def window_rows(s, part, e, cols, width):
            row = lax.broadcasted_iota(jnp.int32, (128, width), 0)
            top = win[s, part, pl.ds(pl.multiple_of(e * 128, 128), 128), cols].astype(F32)
            low = win[s, part, pl.ds(pl.multiple_of(e * 128 + 128, 128), 128), cols].astype(F32)
            return jnp.where(row < 128 - offset, top, low)

        def mix(s):
            def strip(n, carry):
                e = n // 4
                cols = pl.ds(pl.multiple_of(lax.rem(n, 4) * 128, 128), 128)
                rows = pl.ds(pl.multiple_of(e * 128, 128), 128)
                rows_im = pl.ds(pl.multiple_of(size + e * 128, 128), 128)
                w_re, w_im = window_rows(s, 0, e, cols, 128), window_rows(s, 1, e, cols, 128)
                p_re, p_im = waves[s, 0, rows, cols].astype(F32), waves[s, 1, rows, cols].astype(F32)
                upright[rows, cols] = (p_re * w_re - p_im * w_im).astype(BF16)
                upright[rows_im, cols] = (p_re * w_im + p_im * w_re).astype(BF16)
                return carry
            lax.fori_loop(0, 16, strip, 0)

        def forward(s, carry):
            mix(s)
            left(big_m)

            def put(cols, re, im):
                waves[s + 1, 0, :, cols] = re.astype(BF16)
                waves[s + 1, 1, :, cols] = im.astype(BF16)
            right(big_mt, put)
            return carry
        lax.fori_loop(0, slices, forward, 0)

        upright[:size] = waves[slices, 0]
        upright[size:] = waves[slices, 1]
        left(big_f)

        def put_far(cols, re, im):
            excess = re * re + im * im - intensity[:, cols]
            upright[:size, cols] = (excess * re).astype(BF16)
            upright[size:, cols] = (excess * im).astype(BF16)
        right(big_ft, put_far)
        left(big_ft)

        def put_last(cols, re, im):
            far[0, :, cols] = re.astype(BF16)
            far[1, :, cols] = im.astype(BF16)
        right(big_f, put_last)
        flat[:, :size] = far[0]
        flat[:, size:] = far[1]

        def backward(n, carry):
            s = slices - 1 - n

            def put_half(cols, re, im):
                upright[:size, cols] = re.astype(BF16)
                upright[size:, cols] = im.astype(BF16)
            right(big_m, put_half)

            def tile(n, carry):
                cols = pl.ds(pl.multiple_of(n * 256, 256), 256)
                cols_im = pl.ds(pl.multiple_of(size + n * 256, 256), 256)
                got = dot(big_mt[...], upright[:, cols])
                row = lax.broadcasted_iota(jnp.int32, (128, 256), 0)
                head = row < 128 - offset
                last_re = jnp.zeros((128, 256), F32)
                last_im = jnp.zeros((128, 256), F32)
                for e in range(4):
                    g_re = got[e * 128:(e + 1) * 128]
                    g_im = got[size + e * 128:size + (e + 1) * 128]
                    rows = slice(e * 128, (e + 1) * 128)
                    p_re, p_im = waves[s, 0, rows, cols].astype(F32), waves[s, 1, rows, cols].astype(F32)
                    w_re, w_im = window_rows(s, 0, e, cols, 256), window_rows(s, 1, e, cols, 256)
                    o_re = p_re * g_re + p_im * g_im
                    o_im = p_re * g_im - p_im * g_re
                    out[s, e, 0, :, cols] = jnp.where(head, o_re, last_re).astype(BF16)
                    out[s, e, 1, :, cols] = jnp.where(head, o_im, last_im).astype(BF16)
                    last_re, last_im = o_re, o_im
                    flat[rows, cols] = (w_re * g_re + w_im * g_im).astype(BF16)
                    flat[rows, cols_im] = (w_re * g_im - w_im * g_re).astype(BF16)
                out[s, 4, 0, :, cols] = jnp.where(head, 0.0, last_re).astype(BF16)
                out[s, 4, 1, :, cols] = jnp.where(head, 0.0, last_im).astype(BF16)
                return carry
            lax.fori_loop(0, size // 256, tile, 0)
            return carry
        lax.fori_loop(0, slices, backward, 0)


def return_kernel(count, blocks, got, send_sems, recv_sems, self_sem):
    me, cut, parity = place()
    active = (cut // 2) == parity
    barrier = pltpu.get_barrier_semaphore()
    for d in range(REACH):
        for m in range(2):
            def greet():
                pl.semaphore_signal(barrier, inc=1, device_id=worker(me, d, m, count), device_id_type=MESH)
            if d == 2:
                pl.when(cut != 2 * parity + m)(greet)
            else:
                greet()

    def copy_of(d, k):
        return pltpu.make_async_remote_copy(
            src_ref=blocks.at[k, d], dst_ref=got.at[d, lax.rem(cut, 2)],
            send_sem=send_sems.at[k, d], recv_sem=recv_sems.at[d, lax.rem(cut, 2)],
            device_id=(wrapped(me - 2 + d, count), jnp.int32(k)), device_id_type=MESH)

    def local_copy(k):
        return pltpu.make_async_copy(blocks.at[k, 2], got.at[2, lax.rem(cut, 2)], self_sem)

    @pl.when(active)
    def _():
        pl.semaphore_wait(barrier, 19)
        for d in (0, 4, 1, 3, 2):
            for k in range(4):
                if d == 2:
                    pl.when(cut != k)(lambda: copy_of(d, k).start())
                    pl.when(cut == k)(lambda: local_copy(k).start())
                else:
                    copy_of(d, k).start()
        for d in range(REACH):
            for k in range(4):
                if d == 2:
                    pl.when(cut != k)(lambda: copy_of(d, k).wait_send())
                    pl.when(cut == k)(lambda: local_copy(k).wait())
                else:
                    copy_of(d, k).wait_send()

    for d in range(REACH):
        for m in range(2):
            def arrive():
                pltpu.make_async_copy(blocks.at[0, 0], got.at[d, m], recv_sems.at[d, m]).wait()
            if d == 2:
                pl.when(cut != 2 * parity + m)(arrive)
            else:
                arrive()


def add_kernel(pos_ref, got, out, acc):
    width = out.shape[3]
    window = got.shape[4]
    acc[...] = jnp.zeros_like(acc)
    lane = lax.broadcasted_iota(jnp.int32, (4, 8, LANES), 2)
    sub = lax.broadcasted_iota(jnp.int32, (5, 8, LANES), 1)
    count = window // LANES
    zero = jnp.zeros((4, 8, LANES), F32)
    gap = jnp.zeros((1, 8, LANES), F32)
    for d in range(REACH):
        for m in range(2):
            offset = lax.rem(pos_ref[d, 0, 2 * m], 128)
            tile_row, low_row = offset // 8, lax.rem(offset, 8)
            base, shift = column_split(pos_ref[d, 0, 2 * m + 1], width, window)
            turn = lax.rem(shift, LANES)
            keep = lane >= shift
            keep_row = sub >= low_row
            for part in range(2):
                def strip(q, carry):
                    rows = pl.ds(pl.multiple_of(q * 32, 32), 32)
                    turned = [
                        pltpu.roll(
                            got[d, m, part, rows, j * LANES:(j + 1) * LANES].astype(F32).reshape(4, 8, LANES), turn, 2)
                        for j in range(count)
                    ]
                    made = []
                    for j in range(count + 1):
                        here = turned[j] if j < count else zero
                        before = turned[j - 1] if j > 0 else zero
                        moved = pltpu.roll(jnp.where(keep, here, before), low_row, 1)
                        made.append(jnp.where(
                            keep_row, jnp.concatenate([moved, gap]), jnp.concatenate([gap, moved])).reshape(40, LANES))
                    to_rows = pl.ds(pl.multiple_of(tile_row * 8 + q * 32, 8), 40)
                    for j in range(count + 1):
                        to_cols = pl.ds(pl.multiple_of(base + j * LANES, LANES), LANES)
                        acc[part, to_rows, to_cols] += made[j]
                    return carry
                lax.fori_loop(0, 4, strip, 0)
    out[:, 0] = acc[:, :128] + acc[:, 128:]


def local(probe_wave, propagator, object_slices, positions, intensities):
    count = lax.axis_size("scan")
    size = probe_wave.shape[1]
    vmem = pl.BlockSpec(memory_space=pltpu.VMEM)
    smem = pl.BlockSpec(memory_space=pltpu.SMEM)
    anywhere = pl.BlockSpec(memory_space=pl.ANY)
    dma = pltpu.SemaphoreType.DMA
    pos = pl.pallas_call(
        functools.partial(positions_kernel, count),
        out_shape=jax.ShapeDtypeStruct((REACH, 8, LANES), jnp.int32),
        in_specs=[smem],
        out_specs=vmem,
        scratch_shapes=[
            pltpu.VMEM((8, LANES), jnp.int32), pltpu.VMEM((4, 8, LANES), jnp.int32), dma((4,)), dma((4,))],
        compiler_params=pltpu.CompilerParams(
            collective_id=0, has_side_effects=True, vmem_limit_bytes=4 * 2**20),
        name="share_positions",
    )(positions)

    stage = pl.pallas_call(
        pack_kernel,
        out_shape=jax.ShapeDtypeStruct((10, 2, 128, size), BF16),
        in_specs=[smem, vmem],
        out_specs=vmem,
        scratch_shapes=[pltpu.VMEM((2, 256, object_slices.shape[3]), F32)],
        compiler_params=pltpu.CompilerParams(vmem_limit_bytes=24 * 2**20),
        name="pack_windows",
    )(pos, object_slices)

    windows, own_int = pl.pallas_call(
        functools.partial(send_kernel, count),
        out_shape=[
            jax.ShapeDtypeStruct((4, 2, REACH * 128, size), BF16),
            jax.ShapeDtypeStruct((size, size), F32),
        ],
        in_specs=[anywhere, anywhere],
        out_specs=[anywhere, anywhere],
        scratch_shapes=[dma((10,)), dma((4, REACH)), dma, dma, dma],
        compiler_params=pltpu.CompilerParams(
            collective_id=1, has_side_effects=True, vmem_limit_bytes=24 * 2**20),
        name="send_windows",
    )(stage, intensities)

    blocks = pl.pallas_call(
        chain_kernel,
        out_shape=jax.ShapeDtypeStruct((4, REACH, 2, 128, size), BF16),
        in_specs=[smem] + [vmem] * 5,
        out_specs=vmem,
        scratch_shapes=[pltpu.VMEM((2 * size, 2 * size), BF16)] * 4
        + [
            pltpu.VMEM((2 * size, size), BF16),
            pltpu.VMEM((size, 2 * size), BF16),
            pltpu.VMEM((5, 2, size, size), BF16),
            pltpu.VMEM((2, size, size), BF16),
        ],
        compiler_params=pltpu.CompilerParams(vmem_limit_bytes=56 * 2**20),
        name="chain",
    )(pos, windows, probe_wave, propagator, dft_table(size), own_int)

    got = pl.pallas_call(
        functools.partial(return_kernel, count),
        out_shape=jax.ShapeDtypeStruct((REACH, 2, 2, 128, size), BF16),
        in_specs=[anywhere],
        out_specs=anywhere,
        scratch_shapes=[dma((4, REACH)), dma((REACH, 2)), dma],
        compiler_params=pltpu.CompilerParams(
            collective_id=2, has_side_effects=True, vmem_limit_bytes=24 * 2**20),
        name="return_gradients",
    )(blocks)

    return pl.pallas_call(
        add_kernel,
        out_shape=jax.ShapeDtypeStruct(object_slices.shape, F32),
        in_specs=[smem, vmem],
        out_specs=vmem,
        scratch_shapes=[pltpu.VMEM((2, 256, object_slices.shape[3]), F32)],
        compiler_params=pltpu.CompilerParams(vmem_limit_bytes=24 * 2**20),
        name="add_gradients",
    )(pos, got)


def solution(mesh):
    in_specs = (P(), P(), P(None, "cuts", "scan", None), P("scan", None), P("scan", None, None))
    out_specs = P(None, "cuts", "scan", None)
    return jax.shard_map(local, mesh=mesh, in_specs=in_specs, out_specs=out_specs, check_vma=False)
```

time: 738 us -> 158 us (0.21)
  waiting for transfers between devices: 338 us -> 0 us
  local copies, waits for them, and re-layouts: 205 us -> 8.17 us
  Pallas kernels: 0 us -> 147 us
  other arithmetic: 76.2 us -> 0 us
  starting transfers between devices: 59.2 us -> 0 us
  loops' own time: 34.1 us -> 0 us
  matrix products: 20.2 us -> 0 us
    ppermute x18 -> x0, waiting for transfers between devices: 338 us -> none  [the longest x8 226 us: passed_along(): lax.ppermute(shard, axis, [(i, (i + by) % devices) for i in range(devices)])]
    pallas_call x0 -> x6, Pallas kernels: none -> 147 us  [the longest x1 71.7 us: local(): pl.pallas_call(functools.partial(return_kernel, count), out_shape=jax.Sha...]
    dynamic_update_slice x10 -> x0, local copies, waits for them, and re-layouts: 81 us -> none  [backward_turn(): lax.dynamic_update_slice(gradient_sum, current + object_grad, corner)]
    dynamic_slice x34 -> x0, local copies, waits for them, and re-layouts: 59.7 us -> none  [the longest x10 33.7 us: backward_turn(): lax.dynamic_slice(gradient_sum, corner, (2, window_size, window_size))]
    ppermute x18 -> x0, starting transfers between devices: 59.2 us -> none  [the longest x10 49.1 us: shifted(): return lax.ppermute(block, axis, route)]
    another operation x19 -> x0, other arithmetic: 35.2 us -> none
    another operation x13 -> x0, loops' own time: 34.1 us -> none  [the longest x1 18.7 us: local(): lax.fori_loop(0, turn_count, backward_turn, (zero_wave, initial_sum))]
    dot_general x32 -> x0, matrix products: 20.2 us -> none  [the longest x8 8.82 us: complex_product(): jnp.dot(left_im, right_im, preferred_element_type=jnp.float32)]
  transfers between devices with their start and end apart: 18 -> 0, of which waited for: 13 -> 0; matrix products, arithmetic and copies ran while one was open for 25% -> 0% of each run, Pallas kernels for 0% -> 0%
where the time goes in v1:
time: 158 us; the launch traced here: 155 us
  Pallas kernels  147 us (93%)
  local copies, waits for them, and re-layouts  8.17 us (5%)
    pallas_call x1, Pallas kernels, local(): pl.pallas_call(functools.partial(return_kernel, count), out_shape=jax.Sha...  71.7 us
    pallas_call x1, Pallas kernels, local(): pl.pallas_call(functools.partial(send_kernel, count), out_shape=[jax.Shap...  40.2 us
    pallas_call x1, Pallas kernels, local(): pl.pallas_call(add_kernel, out_shape=jax.ShapeDtypeStruct(object_slices.s...  10.7 us
    pallas_call x1, Pallas kernels, local(): pl.pallas_call(functools.partial(positions_kernel, count), out_shape=jax....  9.7 us
    pallas_call x1, Pallas kernels, local(): pl.pallas_call(pack_kernel, out_shape=jax.ShapeDtypeStruct((10, 2, 128, s...  8.27 us
    unnamed x16, local copies, waits for them, and re-layouts  8.17 us
    pallas_call x1, Pallas kernels, local(): pl.pallas_call(chain_kernel, out_shape=jax.ShapeDtypeStruct((4, REACH, 2,...  6.02 us

profile of v1, /device:TPU:1, one launch (start us, length us, event | category | flops | bytes accessed | tf_op | source)
XLA Modules:
  0.0 154.8 jit_solution(10106222939391724159)
XLA Ops:
  0.0 0.0 copy-start.2
  0.0 0.0 copy-start.7
  0.0 0.8 copy-done.7
  0.8 9.7 %share_positions.1.pos_ref = s32[5,8,128]{2,1,0:T(8,128)S(1)} custom-call(s32[2,2]{1,0:T(2,128)S(1)} %copy-done.7), custom_call_target="tpu_custom_call" | custom-call | tf_op jit(solution)/shard_map/share_positions/pallas_call | solution.py:409
  10.5 0.0 copy-start.3
  10.6 1.6 %copy-done.3 = f32[2,1,128,2048]{3,2,1,0:T(8,128)S(1)} copy-done((f32[2,1,128,2048]{3,2,1,0:T(8,128)S(1)}, f32[2,1,128,2048]{3,2,1,0:T(8,128)}, u32[]{:S(2)}) %copy-start.3) | copy-done | bytes 2097176
  12.1 0.0 copy-start.5
  12.1 8.3 %pack_windows.1.stage = bf16[10,2,128,512]{3,2,1,0:T(8,128)(2,1)S(1)} custom-call(s32[5,8,128]{2,1,0:T(8,128)S(1)} %share_positions.1.pos_ref, f32[2,1,128,2048]{3,2,1,0:T(8,128)S(1)} %copy-done.3), custom_call_target="tpu_custom_call" | custom-call | tf_op jit(solution)/shard_map/pack_windows/pallas_call | solution.py:421
  20.4 0.0 copy-done.2
  20.4 40.2 %send_windows.1 = (bf16[4,2,640,512]{3,2,1,0:T(8,128)(2,1)S(1)}, f32[512,512]{1,0:T(8,128)S(1)}) custom-call(bf16[10,2,128,512]{3,2,1,0:T(8,128)(2,1)S(1)} %pack_windows.1.stage, f32[2,512,512]{2,1,0:T(8,128)S(1)} %copy-done.2), custom_call_target="tpu_custom_call" | custom-call | tf_op jit(solution)/shard_map/send_windows/pallas_call | solution.py:431
  60.6 0.0 copy-done.5
  60.6 0.0 copy-start.1
  60.6 2.3 %copy-done.1 = bf16[4,2,640,512]{3,2,1,0:T(8,128)(2,1)} copy-done((bf16[4,2,640,512]{3,2,1,0:T(8,128)(2,1)}, bf16[4,2,640,512]{3,2,1,0:T(8,128)(2,1)S(1)}, u32[]{:S(2)}) %copy-start.1) | copy-done | bytes 5242904
  62.9 0.0 copy-start.4
  62.9 1.0 copy-done.4
  63.9 6.0 %chain.1.blocks = bf16[4,5,2,128,512]{4,3,2,1,0:T(8,128)(2,1)} custom-call(s32[5,8,128]{2,1,0:T(8,128)} %copy-done.5, bf16[4,2,640,512]{3,2,1,0:T(8,128)(2,1)} %copy-done.1, bf16[2,512,512]{2,1,0:T(8,128)(2,1)} %probe.1, bf16[2,512,512]{2,1,0:T(8,128)(2,1)} %prop.1, bf16[2,512,512]{2,1,0:T(8,128)(2,1)} %constant.2.clone.table, f32[512,512]{1,0:T(8,128)} %copy-done.4), custom_call_target="tpu_custom_call" | custom-call | tf_op jit(solution)/shard_map/chain/pallas_call | solution.py:445
  69.9 0.0 copy-start
  69.9 2.5 %copy-done = bf16[4,5,2,128,512]{4,3,2,1,0:T(8,128)(2,1)S(1)} copy-done((bf16[4,5,2,128,512]{4,3,2,1,0:T(8,128)(2,1)S(1)}, bf16[4,5,2,128,512]{4,3,2,1,0:T(8,128)(2,1)}, u32[]{:S(2)}) %copy-start) | copy-done | bytes 5242904
  72.4 0.0 copy-start.6
  72.4 71.7 %return_gradients.1.got = bf16[5,2,2,128,512]{4,3,2,1,0:T(8,128)(2,1)S(1)} custom-call(bf16[4,5,2,128,512]{4,3,2,1,0:T(8,128)(2,1)S(1)} %copy-done), custom_call_target="tpu_custom_call" | custom-call | tf_op jit(solution)/shard_map/return_gradients/pallas_call | solution.py:461
  144.1 0.0 copy-done.6
  144.1 10.7 %add_gradients.1 = f32[2,1,128,2048]{3,2,1,0:T(8,128)} custom-call(s32[5,8,128]{2,1,0:T(8,128)S(1)} %copy-done.6, bf16[5,2,2,128,512]{4,3,2,1,0:T(8,128)(2,1)S(1)} %return_gradients.1.got), custom_call_target="tpu_custom_call" | custom-call | tf_op jit(solution)/shard_map/add_gradients/pallas_call | solution.py:472
Async XLA Ops:
  0.0 20.4 %copy-start.2 = (f32[2,512,512]{2,1,0:T(8,128)S(1)}, f32[2,512,512]{2,1,0:T(8,128)}, u32[]{:S(2)}) copy-start(f32[2,512,512]{2,1,0:T(8,128)} %int_ref.1) | copy-start | bytes 6291460
  0.0 0.8 copy-start.7
  10.5 1.6 %copy-start.3 = (f32[2,1,128,2048]{3,2,1,0:T(8,128)S(1)}, f32[2,1,128,2048]{3,2,1,0:T(8,128)}, u32[]{:S(2)}) copy-start(f32[2,1,128,2048]{3,2,1,0:T(8,128)} %band.1) | copy-start | bytes 6291460
  12.1 48.5 %copy-start.5 = (s32[5,8,128]{2,1,0:T(8,128)}, s32[5,8,128]{2,1,0:T(8,128)S(1)}, u32[]{:S(2)}) copy-start(s32[5,8,128]{2,1,0:T(8,128)S(1)} %share_positions.1.pos_ref) | copy-start | bytes 61444
  60.6 2.3 %copy-start.1 = (bf16[4,2,640,512]{3,2,1,0:T(8,128)(2,1)}, bf16[4,2,640,512]{3,2,1,0:T(8,128)(2,1)S(1)}, u32[]{:S(2)}) copy-start(bf16[4,2,640,512]{3,2,1,0:T(8,128)(2,1)S(1)} %get-tuple-element.7.win) | copy-start | bytes 15728644
  62.9 1.0 copy-start.4
  69.9 2.5 %copy-start = (bf16[4,5,2,128,512]{4,3,2,1,0:T(8,128)(2,1)S(1)}, bf16[4,5,2,128,512]{4,3,2,1,0:T(8,128)(2,1)}, u32[]{:S(2)}) copy-start(bf16[4,5,2,128,512]{4,3,2,1,0:T(8,128)(2,1)} %chain.1.blocks) | copy-start | bytes 15728644
  72.4 71.7 %copy-start.6 = (s32[5,8,128]{2,1,0:T(8,128)S(1)}, s32[5,8,128]{2,1,0:T(8,128)}, u32[]{:S(2)}) copy-start(s32[5,8,128]{2,1,0:T(8,128)} %copy-done.5) | copy-start | bytes 61444

commit v2 on v1

v2 whole, which is shorter than its diff:
```python
import functools
import math

import jax
import jax.numpy as jnp
import numpy as np
from jax import lax
from jax.experimental import pallas as pl
from jax.experimental.pallas import tpu as pltpu
from jax.sharding import PartitionSpec as P

MESH = pl.DeviceIdType.MESH
BF16 = jnp.bfloat16
F32 = jnp.float32
REACH = 5
LANES = 128
ORDER = (0, 4, 1, 3, 2)


def dft_table(length):
    serial = np.arange(length, dtype=np.int32)
    angle_index = serial[:, None] * serial[None, :] % length
    angle = angle_index.astype(np.float32) * np.float32(2.0 * math.pi / length)
    scale = np.float32(1.0 / math.sqrt(length))
    return jnp.asarray(
        np.stack([np.cos(angle) * scale, -np.sin(angle) * scale]), dtype=BF16
    )


def place():
    me = lax.axis_index("scan")
    cut = lax.axis_index("cuts")
    return me, cut, lax.rem(me, 2)


def wrapped(index, count):
    return lax.rem(index + 2 * count, count)


def worker(me, d, m, count):
    band = wrapped(me - d, count)
    return wrapped(me - d + 2, count), 2 * lax.rem(band, 2) + m


def column_split(column, width, window):
    base = jnp.minimum(column // LANES * LANES, width - window - LANES)
    return pl.multiple_of(base, LANES), column - base


def positions_kernel(count, pos_ref, pos_out, tile, pos_in, psend, precv):
    me, cut, parity = place()
    barrier = pltpu.get_barrier_semaphore()
    for d in range(1, REACH):
        pl.semaphore_signal(barrier, inc=1, device_id=(wrapped(me - d, count), cut), device_id_type=MESH)
    lane = lax.broadcasted_iota(jnp.int32, (8, LANES), 1)
    values = jnp.zeros((8, LANES), jnp.int32)
    for n in range(4):
        values = jnp.where(lane == n, pos_ref[n // 2, n % 2], values)
    tile[...] = values
    pos_out[0] = values
    pl.semaphore_wait(barrier, REACH - 1)
    copies = []
    for d in range(1, REACH):
        copy = pltpu.make_async_remote_copy(
            src_ref=tile, dst_ref=pos_in.at[d - 1], send_sem=psend.at[d - 1], recv_sem=precv.at[d - 1],
            device_id=(wrapped(me + d, count), cut), device_id_type=MESH)
        copy.start()
        copies.append(copy)
    for d in range(1, REACH):
        copies[d - 1].wait()
        pos_out[d] = pos_in[d - 1]


def pack_kernel(pos_ref, band, stage, band2):
    window = stage.shape[3]
    width = band.shape[3]
    band2[:, :128] = band[:, 0]
    band2[:, 128:] = band[:, 0]
    lane = lax.broadcasted_iota(jnp.int32, (17, 8, LANES), 2)
    sub = lax.broadcasted_iota(jnp.int32, (16, 8, LANES), 1)
    for d in range(REACH):
        for m in range(2):
            offset = lax.rem(pos_ref[d, 0, 2 * m], 128)
            tile_row, low_row = offset // 8, lax.rem(offset, 8)
            base, shift = column_split(pos_ref[d, 0, 2 * m + 1], width, window)
            turn = lax.rem(LANES - shift, LANES)
            lift = lax.rem(8 - low_row, 8)
            keep = lane + shift < LANES
            keep_row = sub + low_row < 8
            rows = pl.ds(pl.multiple_of(tile_row * 8, 8), 136)
            for part in range(2):
                turned = []
                for j in range(window // LANES + 1):
                    cols = pl.ds(pl.multiple_of(base + j * LANES, LANES), LANES)
                    turned.append(pltpu.roll(band2[part, rows, cols].reshape(17, 8, LANES), turn, 2))
                for j in range(window // LANES):
                    lifted = pltpu.roll(jnp.where(keep, turned[j], turned[j + 1]), lift, 1)
                    made = jnp.where(keep_row, lifted[:16], lifted[1:]).reshape(128, LANES)
                    stage[d * 2 + m, part, :, j * LANES:(j + 1) * LANES] = made.astype(BF16)


def chain_kernel(count, row_ref, stage, int_ref, probe, prop, table, got,
                 win, intensity, out, big_m, big_mt, big_f, big_ft, upright, flat, waves,
                 win_send, win_recv, self_sem, isend, irecv, out_send, out_recv, out_self):
    me, cut, parity = place()
    size = probe.shape[1]
    slices = win.shape[0]
    active = (cut // 2) == parity
    half = lax.rem(cut, 2)

    def owner(d, k):
        return wrapped(me - 2 + d, count), jnp.int32(k)

    def is_self(d, m):
        return cut == 2 * parity + m if d == 2 else None

    def either(same, remote, here):
        if same is None:
            remote()
        else:
            pl.when(jnp.logical_not(same))(remote)
            if here is not None:
                pl.when(same)(here)

    barrier = pltpu.get_barrier_semaphore()

    def greet(device):
        pl.semaphore_signal(barrier, inc=1, device_id=device, device_id_type=MESH)

    for d in range(REACH):
        for m in range(2):
            either(is_self(d, m), lambda: greet(worker(me, d, m, count)), None)

    @pl.when(active)
    def _():
        greet((wrapped(me - 2, count), cut))
        for d in range(REACH):
            for k in range(4):
                either(cut == k if d == 2 else None, lambda: greet(owner(d, k)), None)

    pl.semaphore_wait(barrier, jnp.where(active, 29, 10))

    def window_copy(d, m):
        return pltpu.make_async_remote_copy(
            src_ref=stage.at[d * 2 + m], dst_ref=win.at[cut, :, pl.ds(d * 128, 128), :],
            send_sem=win_send.at[d * 2 + m], recv_sem=win_recv.at[cut, d],
            device_id=worker(me, d, m, count), device_id_type=MESH)

    def window_here(m):
        return pltpu.make_async_copy(stage.at[4 + m], win.at[cut, :, pl.ds(256, 128), :], self_sem)

    def window_arrival(s, d):
        return pltpu.make_async_copy(stage.at[0], win.at[s, :, pl.ds(d * 128, 128), :], win_recv.at[s, d])

    def block_copy(d, k):
        return pltpu.make_async_remote_copy(
            src_ref=out.at[k, d], dst_ref=got.at[d, half],
            send_sem=out_send.at[k, d], recv_sem=out_recv.at[d, half],
            device_id=owner(d, k), device_id_type=MESH)

    def block_here():
        return pltpu.make_async_copy(out.at[cut, 2], got.at[2, half], out_self)

    icopy = pltpu.make_async_remote_copy(
        src_ref=int_ref.at[half], dst_ref=intensity, send_sem=isend, recv_sem=irecv,
        device_id=(wrapped(me + 2, count), cut), device_id_type=MESH)

    for d in ORDER:
        for m in range(2):
            either(is_self(d, m), lambda: window_copy(d, m).start(), lambda: window_here(m).start())

    def dot(a, b):
        return jnp.dot(a, b, preferred_element_type=F32)

    def left(big):
        made = dot(big[...], upright[...])
        flat[:, :size] = made[:size].astype(BF16)
        flat[:, size:] = made[size:].astype(BF16)

    @pl.when(active)
    def _():
        icopy.start()
        offset = lax.rem(row_ref[2, 0, 2 * half], 128)
        for big, big_t, src in ((big_m, big_mt, prop), (big_f, big_ft, table)):
            re, im = src[0], src[1]
            re_t, im_t = re.T, im.T
            big[:size, :size] = re
            big[:size, size:] = -im
            big[size:, :size] = im
            big[size:, size:] = re
            big_t[:size, :size] = re_t
            big_t[:size, size:] = im_t
            big_t[size:, :size] = -im_t
            big_t[size:, size:] = re_t
        waves[0] = probe[...]
        head = lax.broadcasted_iota(jnp.int32, (128, size), 0) < 128 - offset

        def window_rows(s, part, e):
            top = win[s, part, e * 128:(e + 1) * 128, :].astype(F32)
            low = win[s, part, (e + 1) * 128:(e + 2) * 128, :].astype(F32)
            return jnp.where(head, top, low)

        def forward(s, carry):
            for d in range(REACH):
                either(cut == s if d == 2 else None,
                       lambda: window_arrival(s, d).wait(), lambda: window_here(half).wait())
            for e in range(4):
                rows = slice(e * 128, (e + 1) * 128)
                rows_im = slice(size + e * 128, size + (e + 1) * 128)
                w_re, w_im = window_rows(s, 0, e), window_rows(s, 1, e)
                p_re, p_im = waves[s, 0, rows].astype(F32), waves[s, 1, rows].astype(F32)
                upright[rows] = (p_re * w_re - p_im * w_im).astype(BF16)
                upright[rows_im] = (p_re * w_im + p_im * w_re).astype(BF16)
            left(big_m)
            made = dot(flat[...], big_mt[...])
            waves[s + 1, 0] = made[:, :size].astype(BF16)
            waves[s + 1, 1] = made[:, size:].astype(BF16)
            return carry
        lax.fori_loop(0, slices, forward, 0)

        upright[:size] = waves[slices, 0]
        upright[size:] = waves[slices, 1]
        left(big_f)
        icopy.wait()
        made = dot(flat[...], big_ft[...])
        for e in range(4):
            rows = slice(e * 128, (e + 1) * 128)
            re, im = made[rows, :size], made[rows, size:]
            excess = re * re + im * im - intensity[rows]
            upright[rows] = (excess * re).astype(BF16)
            upright[size + e * 128:size + (e + 1) * 128] = (excess * im).astype(BF16)
        left(big_ft)
        flat[...] = dot(flat[...], big_f[...]).astype(BF16)

        def backward(n, carry):
            s = slices - 1 - n
            made = dot(flat[...], big_m[...])
            upright[:size] = made[:, :size].astype(BF16)
            upright[size:] = made[:, size:].astype(BF16)
            made = dot(big_mt[...], upright[...])
            last_re = jnp.zeros((128, size), F32)
            last_im = jnp.zeros((128, size), F32)
            for e in range(4):
                rows = slice(e * 128, (e + 1) * 128)
                g_re, g_im = made[rows], made[size + e * 128:size + (e + 1) * 128]
                p_re, p_im = waves[s, 0, rows].astype(F32), waves[s, 1, rows].astype(F32)
                o_re = p_re * g_re + p_im * g_im
                o_im = p_re * g_im - p_im * g_re
                out[s, e, 0] = jnp.where(head, o_re, last_re).astype(BF16)
                out[s, e, 1] = jnp.where(head, o_im, last_im).astype(BF16)
                last_re, last_im = o_re, o_im
                w_re, w_im = window_rows(s, 0, e), window_rows(s, 1, e)
                flat[rows, :size] = (w_re * g_re + w_im * g_im).astype(BF16)
                flat[rows, size:] = (w_re * g_im - w_im * g_re).astype(BF16)
            out[s, 4, 0] = jnp.where(head, 0.0, last_re).astype(BF16)
            out[s, 4, 1] = jnp.where(head, 0.0, last_im).astype(BF16)
            for d in ORDER:
                either(cut == s if d == 2 else None,
                       lambda: block_copy(d, s).start(), lambda: block_here().start())
            return carry
        lax.fori_loop(0, slices, backward, 0)

    for d in range(REACH):
        for m in range(2):
            either(is_self(d, m), lambda: window_copy(d, m).wait_send(), None)

    @pl.when(active)
    def _():
        for d in range(REACH):
            for k in range(4):
                either(cut == k if d == 2 else None,
                       lambda: block_copy(d, k).wait_send(), lambda: block_here().wait())

    for d in range(REACH):
        for m in range(2):
            either(is_self(d, m),
                   lambda: pltpu.make_async_copy(out.at[0, 0], got.at[d, m], out_recv.at[d, m]).wait(), None)


def add_kernel(pos_ref, got, out, acc):
    width = out.shape[3]
    window = got.shape[4]
    acc[...] = jnp.zeros_like(acc)
    lane = lax.broadcasted_iota(jnp.int32, (16, 8, LANES), 2)
    sub = lax.broadcasted_iota(jnp.int32, (17, 8, LANES), 1)
    count = window // LANES
    zero = jnp.zeros((16, 8, LANES), F32)
    gap = jnp.zeros((1, 8, LANES), F32)
    for d in range(REACH):
        for m in range(2):
            offset = lax.rem(pos_ref[d, 0, 2 * m], 128)
            tile_row, low_row = offset // 8, lax.rem(offset, 8)
            base, shift = column_split(pos_ref[d, 0, 2 * m + 1], width, window)
            turn = lax.rem(shift, LANES)
            keep = lane >= shift
            keep_row = sub >= low_row
            to_rows = pl.ds(pl.multiple_of(tile_row * 8, 8), 136)
            for part in range(2):
                before = zero
                for j in range(count + 1):
                    here = zero
                    if j < count:
                        here = pltpu.roll(
                            got[d, m, part, :, j * LANES:(j + 1) * LANES].astype(F32).reshape(16, 8, LANES), turn, 2)
                    moved = pltpu.roll(jnp.where(keep, here, before), low_row, 1)
                    before = here
                    made = jnp.where(keep_row, jnp.concatenate([moved, gap]), jnp.concatenate([gap, moved]))
                    to_cols = pl.ds(pl.multiple_of(base + j * LANES, LANES), LANES)
                    acc[part, to_rows, to_cols] += made.reshape(136, LANES)
    out[:, 0] = acc[:, :128] + acc[:, 128:]


def local(probe_wave, propagator, object_slices, positions, intensities):
    count = lax.axis_size("scan")
    size = probe_wave.shape[1]
    vmem = pl.BlockSpec(memory_space=pltpu.VMEM)
    smem = pl.BlockSpec(memory_space=pltpu.SMEM)
    anywhere = pl.BlockSpec(memory_space=pl.ANY)
    dma = pltpu.SemaphoreType.DMA
    pos = pl.pallas_call(
        functools.partial(positions_kernel, count),
        out_shape=jax.ShapeDtypeStruct((REACH, 8, LANES), jnp.int32),
        in_specs=[smem],
        out_specs=vmem,
        scratch_shapes=[
            pltpu.VMEM((8, LANES), jnp.int32), pltpu.VMEM((4, 8, LANES), jnp.int32), dma((4,)), dma((4,))],
        compiler_params=pltpu.CompilerParams(
            collective_id=0, has_side_effects=True, vmem_limit_bytes=4 * 2**20),
        name="share_positions",
    )(positions)

    stage = pl.pallas_call(
        pack_kernel,
        out_shape=jax.ShapeDtypeStruct((10, 2, 128, size), BF16),
        in_specs=[smem, vmem],
        out_specs=vmem,
        scratch_shapes=[pltpu.VMEM((2, 256, object_slices.shape[3]), F32)],
        compiler_params=pltpu.CompilerParams(vmem_limit_bytes=24 * 2**20),
        name="pack_windows",
    )(pos, object_slices)

    got = pl.pallas_call(
        functools.partial(chain_kernel, count),
        out_shape=jax.ShapeDtypeStruct((REACH, 2, 2, 128, size), BF16),
        in_specs=[smem, vmem, anywhere, vmem, vmem, vmem],
        out_specs=anywhere,
        scratch_shapes=[
            pltpu.VMEM((4, 2, REACH * 128, size), BF16),
            pltpu.VMEM((size, size), F32),
            pltpu.VMEM((4, REACH, 2, 128, size), BF16),
        ]
        + [pltpu.VMEM((2 * size, 2 * size), BF16)] * 4
        + [
            pltpu.VMEM((2 * size, size), BF16),
            pltpu.VMEM((size, 2 * size), BF16),
            pltpu.VMEM((5, 2, size, size), BF16),
            dma((10,)), dma((4, REACH)), dma, dma, dma, dma((4, REACH)), dma((REACH, 2)), dma,
        ],
        compiler_params=pltpu.CompilerParams(
            collective_id=1, has_side_effects=True, vmem_limit_bytes=52 * 2**20),
        name="chain",
    )(pos, stage, intensities, probe_wave, propagator, dft_table(size))

    return pl.pallas_call(
        add_kernel,
        out_shape=jax.ShapeDtypeStruct(object_slices.shape, F32),
        in_specs=[smem, vmem],
        out_specs=vmem,
        scratch_shapes=[pltpu.VMEM((2, 256, object_slices.shape[3]), F32)],
        compiler_params=pltpu.CompilerParams(vmem_limit_bytes=24 * 2**20),
        name="add_gradients",
    )(pos, got)


def solution(mesh):
    in_specs = (P(), P(), P(None, "cuts", "scan", None), P("scan", None), P("scan", None, None))
    out_specs = P(None, "cuts", "scan", None)
    return jax.shard_map(local, mesh=mesh, in_specs=in_specs, out_specs=out_specs, check_vma=False)
```

time: 158 us -> 118 us (0.75); the launches traced: 155 us -> 117 us
  Pallas kernels: 147 us -> 112 us
  local copies, waits for them, and re-layouts: 8.17 us -> 5.49 us
    pallas_call x3 -> x1, Pallas kernels: 118 us -> 95.4 us  [local(): pl.pallas_call(functools.partial(chain_kernel, count), out_shape=jax.Shap...]
    pallas_call x1, Pallas kernels: 10.7 us -> 4.43 us  [local(): pl.pallas_call(add_kernel, out_shape=jax.ShapeDtypeStruct(object_slices.s...]
    pallas_call x1, Pallas kernels: 8.27 us -> 2.33 us  [local(): pl.pallas_call(pack_kernel, out_shape=jax.ShapeDtypeStruct((10, 2, 128, s...]
    unnamed x16 -> x10, local copies, waits for them, and re-layouts: 8.17 us -> 5.49 us
where the time goes in v2:
time: 118 us; the launch traced here: 117 us
  Pallas kernels  112 us (95%)
  local copies, waits for them, and re-layouts  5.49 us (5%)
    pallas_call x1, Pallas kernels, local(): pl.pallas_call(functools.partial(chain_kernel, count), out_shape=jax.Shap...  95.4 us
    pallas_call x1, Pallas kernels, local(): pl.pallas_call(functools.partial(positions_kernel, count), out_shape=jax....  9.7 us
    unnamed x10, local copies, waits for them, and re-layouts  5.49 us
    pallas_call x1, Pallas kernels, local(): pl.pallas_call(add_kernel, out_shape=jax.ShapeDtypeStruct(object_slices.s...  4.43 us

profile of v2, /device:TPU:1, one launch (start us, length us, event | category | flops | bytes accessed | tf_op | source)
XLA Modules:
  0.0 117.4 jit_solution(17738273598845820353)
XLA Ops:
  0.0 0.0 copy-start.4
  0.0 0.7 copy-done.4
  0.7 9.7 %share_positions.1.pos_ref.row_ref = s32[5,8,128]{2,1,0:T(8,128)S(1)} custom-call(s32[2,2]{1,0:T(2,128)S(1)} %copy-done.4), custom_call_target="tpu_custom_call" | custom-call | tf_op jit(solution)/shard_map/share_positions/pallas_call | solution.py:320
  10.4 0.0 copy-start.2
  10.4 1.6 %copy-done.2 = f32[2,1,128,2048]{3,2,1,0:T(8,128)S(1)} copy-done((f32[2,1,128,2048]{3,2,1,0:T(8,128)S(1)}, f32[2,1,128,2048]{3,2,1,0:T(8,128)}, u32[]{:S(2)}) %copy-start.2) | copy-done | bytes 2097176
  12.0 0.0 copy-start.3
  12.0 2.3 %pack_windows.1.stage = bf16[10,2,128,512]{3,2,1,0:T(8,128)(2,1)S(1)} custom-call(s32[5,8,128]{2,1,0:T(8,128)S(1)} %share_positions.1.pos_ref.row_ref, f32[2,1,128,2048]{3,2,1,0:T(8,128)S(1)} %copy-done.2), custom_call_target="tpu_custom_call" | custom-call | tf_op jit(solution)/shard_map/pack_windows/pallas_call | solution.py:332
  14.3 0.0 copy-start.1
  14.3 1.5 %copy-done.1 = bf16[10,2,128,512]{3,2,1,0:T(8,128)(2,1)} copy-done((bf16[10,2,128,512]{3,2,1,0:T(8,128)(2,1)}, bf16[10,2,128,512]{3,2,1,0:T(8,128)(2,1)S(1)}, u32[]{:S(2)}) %copy-start.1) | copy-done | bytes 2621464
  15.8 0.0 copy-done.3
  15.8 95.4 %chain.1.got = bf16[5,2,2,128,512]{4,3,2,1,0:T(8,128)(2,1)} custom-call(s32[5,8,128]{2,1,0:T(8,128)S(1)} %share_positions.1.pos_ref.row_ref, bf16[10,2,128,512]{3,2,1,0:T(8,128)(2,1)} %copy-done.1, f32[2,512,512]{2,1,0:T(8,128)} %int_ref.1, bf16[2,512,512]{2,1,0:T(8,128)(2,1)S(1)} %copy-done.3, bf16[2,512,512]{2,1,0:T(8,128)(2,1)} %prop.1, ...), custom_call_target="tpu_custom_call" | custom-call | tf_op jit(solution)/shard_map/chain/pallas_call | solution.py:342
  111.3 0.0 copy-start
  111.3 1.7 %copy-done = bf16[5,2,2,128,512]{4,3,2,1,0:T(8,128)(2,1)S(1)} copy-done((bf16[5,2,2,128,512]{4,3,2,1,0:T(8,128)(2,1)S(1)}, bf16[5,2,2,128,512]{4,3,2,1,0:T(8,128)(2,1)}, u32[]{:S(2)}) %copy-start) | copy-done | bytes 2621464
  113.0 4.4 %add_gradients.1 = f32[2,1,128,2048]{3,2,1,0:T(8,128)} custom-call(s32[5,8,128]{2,1,0:T(8,128)S(1)} %share_positions.1.pos_ref.row_ref, bf16[5,2,2,128,512]{4,3,2,1,0:T(8,128)(2,1)S(1)} %copy-done), custom_call_target="tpu_custom_call" | custom-call | tf_op jit(solution)/shard_map/add_gradients/pallas_call | solution.py:364
Async XLA Ops:
  0.0 0.7 copy-start.4
  10.4 1.6 %copy-start.2 = (f32[2,1,128,2048]{3,2,1,0:T(8,128)S(1)}, f32[2,1,128,2048]{3,2,1,0:T(8,128)}, u32[]{:S(2)}) copy-start(f32[2,1,128,2048]{3,2,1,0:T(8,128)} %band.1) | copy-start | bytes 6291460
  12.0 3.8 %copy-start.3 = (bf16[2,512,512]{2,1,0:T(8,128)(2,1)S(1)}, bf16[2,512,512]{2,1,0:T(8,128)(2,1)}, u32[]{:S(2)}) copy-start(bf16[2,512,512]{2,1,0:T(8,128)(2,1)} %probe.1) | copy-start | bytes 3145732
  14.3 1.5 %copy-start.1 = (bf16[10,2,128,512]{3,2,1,0:T(8,128)(2,1)}, bf16[10,2,128,512]{3,2,1,0:T(8,128)(2,1)S(1)}, u32[]{:S(2)}) copy-start(bf16[10,2,128,512]{3,2,1,0:T(8,128)(2,1)S(1)} %pack_windows.1.stage) | copy-start | bytes 7864324
  111.3 1.7 %copy-start = (bf16[5,2,2,128,512]{4,3,2,1,0:T(8,128)(2,1)S(1)}, bf16[5,2,2,128,512]{4,3,2,1,0:T(8,128)(2,1)}, u32[]{:S(2)}) copy-start(bf16[5,2,2,128,512]{4,3,2,1,0:T(8,128)(2,1)} %chain.1.got) | copy-start | bytes 7864324

commit v3 on v2

--- a/solution.py
+++ b/solution.py
@@ -14,7 +14,6 @@
 F32 = jnp.float32
 REACH = 5
 LANES = 128
-ORDER = (0, 4, 1, 3, 2)
 
 
 def dft_table(length):
@@ -71,11 +70,17 @@
         pos_out[d] = pos_in[d - 1]
 
 
-def pack_kernel(pos_ref, band, stage, band2):
+def pack_kernel(pos_ref, band, stage, band2, load_sem):
     window = stage.shape[3]
     width = band.shape[3]
-    band2[:, :128] = band[:, 0]
-    band2[:, 128:] = band[:, 0]
+    loads = [
+        pltpu.make_async_copy(band.at[:, 0], band2.at[:, pl.ds(h * 128, 128), :], load_sem.at[h])
+        for h in range(2)
+    ]
+    for load in loads:
+        load.start()
+    for load in loads:
+        load.wait()
     lane = lax.broadcasted_iota(jnp.int32, (17, 8, LANES), 2)
     sub = lax.broadcasted_iota(jnp.int32, (16, 8, LANES), 1)
     for d in range(REACH):
@@ -99,14 +104,17 @@
                     stage[d * 2 + m, part, :, j * LANES:(j + 1) * LANES] = made.astype(BF16)
 
 
-def chain_kernel(count, row_ref, stage, int_ref, probe, prop, table, got,
-                 win, intensity, out, big_m, big_mt, big_f, big_ft, upright, flat, waves,
-                 win_send, win_recv, self_sem, isend, irecv, out_send, out_recv, out_self):
+def chain_kernel(count, row_ref, stage, int_ref, probe_ref, prop_ref, table_ref, got,
+                 win, intensity, out, edge, cross, back, prop, table,
+                 big_m, big_mt, big_f, big_ft, upright, flat, waves,
+                 load_sem, win_send, win_recv, self_sem, edge_send, edge_recv, cross_send, cross_self,
+                 isend, irecv, out_send, out_recv, out_self, back_send, back_recv, back_self, last_send):
     me, cut, parity = place()
-    size = probe.shape[1]
+    size = flat.shape[0]
     slices = win.shape[0]
     active = (cut // 2) == parity
     half = lax.rem(cut, 2)
+    behind, ahead = wrapped(me - 2, count), wrapped(me + 2, count)
 
     def owner(d, k):
         return wrapped(me - 2 + d, count), jnp.int32(k)
@@ -122,35 +130,62 @@
             if here is not None:
                 pl.when(same)(here)
 
+    loads = [
+        pltpu.make_async_copy(src, dst, load_sem.at[n])
+        for n, (src, dst) in enumerate(((probe_ref, waves.at[0]), (prop_ref, prop), (table_ref, table)))
+    ]
+    for load in loads:
+        load.start()
+
     barrier = pltpu.get_barrier_semaphore()
 
     def greet(device):
         pl.semaphore_signal(barrier, inc=1, device_id=device, device_id_type=MESH)
 
-    for d in range(REACH):
-        for m in range(2):
+    greet((behind, cut))
+    greet((ahead, cut))
+    for m in range(2):
+        for d in (1, 2, 3):
             either(is_self(d, m), lambda: greet(worker(me, d, m, count)), None)
+        either(is_self(2, m), lambda: greet(worker(me, 2, m, count)), None)
 
     @pl.when(active)
     def _():
-        greet((wrapped(me - 2, count), cut))
-        for d in range(REACH):
-            for k in range(4):
+        for k in range(4):
+            for d in (1, 2, 3):
                 either(cut == k if d == 2 else None, lambda: greet(owner(d, k)), None)
-
-    pl.semaphore_wait(barrier, jnp.where(active, 29, 10))
+            either(cut == k, lambda: greet(owner(2, k)), None)
+
+    pl.semaphore_wait(barrier, jnp.where(active, 22, 10))
+
+    def unit(s, e):
+        return win.at[s, :, pl.ds(e * 128, 128), :]
 
     def window_copy(d, m):
         return pltpu.make_async_remote_copy(
-            src_ref=stage.at[d * 2 + m], dst_ref=win.at[cut, :, pl.ds(d * 128, 128), :],
+            src_ref=stage.at[d * 2 + m], dst_ref=unit(cut, d),
             send_sem=win_send.at[d * 2 + m], recv_sem=win_recv.at[cut, d],
             device_id=worker(me, d, m, count), device_id_type=MESH)
 
     def window_here(m):
-        return pltpu.make_async_copy(stage.at[4 + m], win.at[cut, :, pl.ds(256, 128), :], self_sem)
-
-    def window_arrival(s, d):
-        return pltpu.make_async_copy(stage.at[0], win.at[s, :, pl.ds(d * 128, 128), :], win_recv.at[s, d])
+        return pltpu.make_async_copy(stage.at[4 + m], unit(cut, 2), self_sem)
+
+    def edge_copy(n):
+        return pltpu.make_async_remote_copy(
+            src_ref=stage.at[pl.ds(8 * n, 2)], dst_ref=edge.at[n],
+            send_sem=edge_send.at[n], recv_sem=edge_recv.at[n],
+            device_id=((ahead, behind)[n], cut), device_id_type=MESH)
+
+    def cross_copy(m):
+        return pltpu.make_async_remote_copy(
+            src_ref=cross.at[m], dst_ref=unit(cut, 0), send_sem=cross_send.at[m], recv_sem=win_recv.at[cut, 0],
+            device_id=(me, 2 * parity + m), device_id_type=MESH)
+
+    def cross_here(m):
+        return pltpu.make_async_copy(cross.at[m], unit(cut, 0), cross_self)
+
+    def window_arrival(s, e):
+        return pltpu.make_async_copy(stage.at[0], unit(s, e), win_recv.at[s, e])
 
     def block_copy(d, k):
         return pltpu.make_async_remote_copy(
@@ -161,11 +196,26 @@
     def block_here():
         return pltpu.make_async_copy(out.at[cut, 2], got.at[2, half], out_self)
 
+    def back_copy(k):
+        return pltpu.make_async_remote_copy(
+            src_ref=out.at[k, 0], dst_ref=back.at[half], send_sem=back_send.at[k], recv_sem=back_recv.at[half],
+            device_id=(me, jnp.int32(k)), device_id_type=MESH)
+
+    def back_here():
+        return pltpu.make_async_copy(out.at[cut, 0], back.at[half], back_self)
+
+    def last_copy(m, n):
+        return pltpu.make_async_remote_copy(
+            src_ref=back.at[m], dst_ref=got.at[4 * n, m], send_sem=last_send.at[m, n], recv_sem=out_recv.at[4 * n, m],
+            device_id=((behind, ahead)[n], cut), device_id_type=MESH)
+
     icopy = pltpu.make_async_remote_copy(
         src_ref=int_ref.at[half], dst_ref=intensity, send_sem=isend, recv_sem=irecv,
-        device_id=(wrapped(me + 2, count), cut), device_id_type=MESH)
-
-    for d in ORDER:
+        device_id=(ahead, cut), device_id_type=MESH)
+
+    for n in range(2):
+        edge_copy(n).start()
+    for d in (1, 3, 2):
         for m in range(2):
             either(is_self(d, m), lambda: window_copy(d, m).start(), lambda: window_here(m).start())
 
@@ -176,6 +226,17 @@
         made = dot(big[...], upright[...])
         flat[:, :size] = made[:size].astype(BF16)
         flat[:, size:] = made[size:].astype(BF16)
+
+    for load in loads:
+        load.wait()
+    for n in range(2):
+        edge_copy(n).wait_recv()
+    for m in range(2):
+        low = lax.broadcasted_iota(jnp.int32, (128, size), 0) < 128 - lax.rem(row_ref[2, 0, 2 * m], 128)
+        for part in range(2):
+            cross[m, part] = jnp.where(
+                low, edge[0, m, part].astype(F32), edge[1, m, part].astype(F32)).astype(BF16)
+        either(is_self(2, m), lambda: cross_copy(m).start(), lambda: cross_here(m).start())
 
     @pl.when(active)
     def _():
@@ -192,18 +253,22 @@
             big_t[:size, size:] = im_t
             big_t[size:, :size] = -im_t
             big_t[size:, size:] = re_t
-        waves[0] = probe[...]
         head = lax.broadcasted_iota(jnp.int32, (128, size), 0) < 128 - offset
 
         def window_rows(s, part, e):
             top = win[s, part, e * 128:(e + 1) * 128, :].astype(F32)
-            low = win[s, part, (e + 1) * 128:(e + 2) * 128, :].astype(F32)
+            after = (e + 1) % 4
+            low = win[s, part, after * 128:(after + 1) * 128, :].astype(F32)
             return jnp.where(head, top, low)
 
         def forward(s, carry):
-            for d in range(REACH):
-                either(cut == s if d == 2 else None,
-                       lambda: window_arrival(s, d).wait(), lambda: window_here(half).wait())
+            for e in range(4):
+                same, here = None, None
+                if e == 0:
+                    same, here = cut == s, lambda: cross_here(half).wait()
+                elif e == 2:
+                    same, here = cut == s, lambda: window_here(half).wait()
+                either(same, lambda: window_arrival(s, e).wait(), here)
             for e in range(4):
                 rows = slice(e * 128, (e + 1) * 128)
                 rows_im = slice(size + e * 128, size + (e + 1) * 128)
@@ -238,60 +303,83 @@
             upright[:size] = made[:, :size].astype(BF16)
             upright[size:] = made[:, size:].astype(BF16)
             made = dot(big_mt[...], upright[...])
-            last_re = jnp.zeros((128, size), F32)
-            last_im = jnp.zeros((128, size), F32)
+            terms = []
             for e in range(4):
                 rows = slice(e * 128, (e + 1) * 128)
                 g_re, g_im = made[rows], made[size + e * 128:size + (e + 1) * 128]
                 p_re, p_im = waves[s, 0, rows].astype(F32), waves[s, 1, rows].astype(F32)
-                o_re = p_re * g_re + p_im * g_im
-                o_im = p_re * g_im - p_im * g_re
-                out[s, e, 0] = jnp.where(head, o_re, last_re).astype(BF16)
-                out[s, e, 1] = jnp.where(head, o_im, last_im).astype(BF16)
-                last_re, last_im = o_re, o_im
+                terms.append((p_re * g_re + p_im * g_im, p_re * g_im - p_im * g_re))
+            for e in range(4):
+                for part in range(2):
+                    out[s, e, part] = jnp.where(head, terms[e][part], terms[e - 1][part]).astype(BF16)
+            either(cut == s, lambda: back_copy(s).start(), lambda: back_here().start())
+            for d in (1, 3, 2):
+                either(cut == s if d == 2 else None,
+                       lambda: block_copy(d, s).start(), lambda: block_here().start())
+            for e in range(4):
+                rows = slice(e * 128, (e + 1) * 128)
+                g_re, g_im = made[rows], made[size + e * 128:size + (e + 1) * 128]
                 w_re, w_im = window_rows(s, 0, e), window_rows(s, 1, e)
                 flat[rows, :size] = (w_re * g_re + w_im * g_im).astype(BF16)
                 flat[rows, size:] = (w_re * g_im - w_im * g_re).astype(BF16)
-            out[s, 4, 0] = jnp.where(head, 0.0, last_re).astype(BF16)
-            out[s, 4, 1] = jnp.where(head, 0.0, last_im).astype(BF16)
-            for d in ORDER:
-                either(cut == s if d == 2 else None,
-                       lambda: block_copy(d, s).start(), lambda: block_here().start())
             return carry
         lax.fori_loop(0, slices, backward, 0)
 
-    for d in range(REACH):
-        for m in range(2):
+    for m in range(2):
+        either(is_self(2, m),
+               lambda: pltpu.make_async_copy(out.at[0, 0], back.at[m], back_recv.at[m]).wait(),
+               lambda: back_here().wait())
+        for n in range(2):
+            last_copy(m, n).start()
+
+    for n in range(2):
+        edge_copy(n).wait_send()
+    for m in range(2):
+        either(is_self(2, m), lambda: cross_copy(m).wait_send(), None)
+        for d in (1, 2, 3):
             either(is_self(d, m), lambda: window_copy(d, m).wait_send(), None)
 
     @pl.when(active)
     def _():
-        for d in range(REACH):
-            for k in range(4):
+        for k in range(4):
+            either(cut == k, lambda: back_copy(k).wait_send(), None)
+            for d in (1, 2, 3):
                 either(cut == k if d == 2 else None,
                        lambda: block_copy(d, k).wait_send(), lambda: block_here().wait())
 
-    for d in range(REACH):
-        for m in range(2):
+    for m in range(2):
+        for d in range(REACH):
             either(is_self(d, m),
                    lambda: pltpu.make_async_copy(out.at[0, 0], got.at[d, m], out_recv.at[d, m]).wait(), None)
-
-
-def add_kernel(pos_ref, got, out, acc):
+        for n in range(2):
+            last_copy(m, n).wait_send()
+
+
+def add_kernel(pos_ref, got_ref, out, acc, got, load_sem):
     width = out.shape[3]
     window = got.shape[4]
+    loads = [pltpu.make_async_copy(got_ref.at[d], got.at[d], load_sem.at[d]) for d in range(REACH)]
+    for load in loads:
+        load.start()
     acc[...] = jnp.zeros_like(acc)
+    row = 8 * lax.broadcasted_iota(jnp.int32, (16, 8, LANES), 0) + lax.broadcasted_iota(jnp.int32, (16, 8, LANES), 1)
     lane = lax.broadcasted_iota(jnp.int32, (16, 8, LANES), 2)
     sub = lax.broadcasted_iota(jnp.int32, (17, 8, LANES), 1)
     count = window // LANES
     zero = jnp.zeros((16, 8, LANES), F32)
     gap = jnp.zeros((1, 8, LANES), F32)
     for d in range(REACH):
+        loads[d].wait()
         for m in range(2):
             offset = lax.rem(pos_ref[d, 0, 2 * m], 128)
             tile_row, low_row = offset // 8, lax.rem(offset, 8)
             base, shift = column_split(pos_ref[d, 0, 2 * m + 1], width, window)
             turn = lax.rem(shift, LANES)
+            mine = None
+            if d == 0:
+                mine = row < 128 - offset
+            elif d == REACH - 1:
+                mine = row >= 128 - offset
             keep = lane >= shift
             keep_row = sub >= low_row
             to_rows = pl.ds(pl.multiple_of(tile_row * 8, 8), 136)
@@ -300,8 +388,10 @@
                 for j in range(count + 1):
                     here = zero
                     if j < count:
-                        here = pltpu.roll(
-                            got[d, m, part, :, j * LANES:(j + 1) * LANES].astype(F32).reshape(16, 8, LANES), turn, 2)
+                        here = got[d, m, part, :, j * LANES:(j + 1) * LANES].astype(F32).reshape(16, 8, LANES)
+                        if mine is not None:
+                            here = jnp.where(mine, here, 0.0)
+                        here = pltpu.roll(here, turn, 2)
                     moved = pltpu.roll(jnp.where(keep, here, before), low_row, 1)
                     before = here
                     made = jnp.where(keep_row, jnp.concatenate([moved, gap]), jnp.concatenate([gap, moved]))
@@ -332,9 +422,9 @@
     stage = pl.pallas_call(
         pack_kernel,
         out_shape=jax.ShapeDtypeStruct((10, 2, 128, size), BF16),
-        in_specs=[smem, vmem],
+        in_specs=[smem, anywhere],
         out_specs=vmem,
-        scratch_shapes=[pltpu.VMEM((2, 256, object_slices.shape[3]), F32)],
+        scratch_shapes=[pltpu.VMEM((2, 256, object_slices.shape[3]), F32), dma((2,))],
         compiler_params=pltpu.CompilerParams(vmem_limit_bytes=24 * 2**20),
         name="pack_windows",
     )(pos, object_slices)
@@ -342,19 +432,25 @@
     got = pl.pallas_call(
         functools.partial(chain_kernel, count),
         out_shape=jax.ShapeDtypeStruct((REACH, 2, 2, 128, size), BF16),
-        in_specs=[smem, vmem, anywhere, vmem, vmem, vmem],
+        in_specs=[smem, vmem, anywhere, anywhere, anywhere, anywhere],
         out_specs=anywhere,
         scratch_shapes=[
-            pltpu.VMEM((4, 2, REACH * 128, size), BF16),
+            pltpu.VMEM((4, 2, size, size), BF16),
             pltpu.VMEM((size, size), F32),
-            pltpu.VMEM((4, REACH, 2, 128, size), BF16),
+            pltpu.VMEM((4, 4, 2, 128, size), BF16),
+            pltpu.VMEM((2, 2, 2, 128, size), BF16),
+            pltpu.VMEM((2, 2, 128, size), BF16),
+            pltpu.VMEM((2, 2, 128, size), BF16),
+            pltpu.VMEM((2, size, size), BF16),
+            pltpu.VMEM((2, size, size), BF16),
         ]
         + [pltpu.VMEM((2 * size, 2 * size), BF16)] * 4
         + [
             pltpu.VMEM((2 * size, size), BF16),
             pltpu.VMEM((size, 2 * size), BF16),
             pltpu.VMEM((5, 2, size, size), BF16),
-            dma((10,)), dma((4, REACH)), dma, dma, dma, dma((4, REACH)), dma((REACH, 2)), dma,
+            dma((3,)), dma((10,)), dma((4, 4)), dma, dma((2,)), dma((2,)), dma((2,)), dma,
+            dma, dma, dma((4, 4)), dma((REACH, 2)), dma, dma((4,)), dma((2,)), dma, dma((2, 2)),
         ],
         compiler_params=pltpu.CompilerParams(
             collective_id=1, has_side_effects=True, vmem_limit_bytes=52 * 2**20),
@@ -364,9 +460,10 @@
     return pl.pallas_call(
         add_kernel,
         out_shape=jax.ShapeDtypeStruct(object_slices.shape, F32),
-        in_specs=[smem, vmem],
+        in_specs=[smem, anywhere],
         out_specs=vmem,
-        scratch_shapes=[pltpu.VMEM((2, 256, object_slices.shape[3]), F32)],
+        scratch_shapes=[
+            pltpu.VMEM((2, 256, object_slices.shape[3]), F32), pltpu.VMEM(got.shape, BF16), dma((REACH,))],
         compiler_params=pltpu.CompilerParams(vmem_limit_bytes=24 * 2**20),
         name="add_gradients",
     )(pos, got)

time: 118 us -> 110 us (0.932)
  Pallas kernels: 112 us -> 104 us
    pallas_call x1, Pallas kernels: 95.4 us -> 86.6 us  [local(): pl.pallas_call(functools.partial(chain_kernel, count), out_shape=jax.Shap...]
where the time goes in v3:
time: 110 us; the launch traced here: 109 us
  Pallas kernels  104 us (95%)
  local copies, waits for them, and re-layouts  5.49 us (5%)
    pallas_call x1, Pallas kernels, local(): pl.pallas_call(functools.partial(chain_kernel, count), out_shape=jax.Shap...  86.6 us
    pallas_call x1, Pallas kernels, local(): pl.pallas_call(functools.partial(positions_kernel, count), out_shape=jax....  9.7 us
    unnamed x10, local copies, waits for them, and re-layouts  5.49 us
    pallas_call x1, Pallas kernels, local(): pl.pallas_call(add_kernel, out_shape=jax.ShapeDtypeStruct(object_slices.s...  5.01 us
    pallas_call x1, Pallas kernels, local(): pl.pallas_call(pack_kernel, out_shape=jax.ShapeDtypeStruct((10, 2, 128, s...  2.38 us

profile of v3, /device:TPU:1, one launch (start us, length us, event | category | flops | bytes accessed | tf_op | source)
XLA Modules:
  0.0 109.4 jit_solution(3286664397374017394)
XLA Ops:
  0.0 0.0 copy-start.4
  0.0 0.7 copy-done.4
  0.7 9.7 %share_positions.1.pos_ref.row_ref = s32[5,8,128]{2,1,0:T(8,128)S(1)} custom-call(s32[2,2]{1,0:T(2,128)S(1)} %copy-done.4), custom_call_target="tpu_custom_call" | custom-call | tf_op jit(solution)/shard_map/share_positions/pallas_call | solution.py:410
  10.4 0.0 copy-start.2
  10.4 1.6 %copy-done.2 = f32[2,1,128,2048]{3,2,1,0:T(8,128)S(1)} copy-done((f32[2,1,128,2048]{3,2,1,0:T(8,128)S(1)}, f32[2,1,128,2048]{3,2,1,0:T(8,128)}, u32[]{:S(2)}) %copy-start.2) | copy-done | bytes 2097176
  12.0 0.0 copy-start.3
  12.0 2.4 %pack_windows.1.stage = bf16[10,2,128,512]{3,2,1,0:T(8,128)(2,1)S(1)} custom-call(s32[5,8,128]{2,1,0:T(8,128)S(1)} %share_positions.1.pos_ref.row_ref, f32[2,1,128,2048]{3,2,1,0:T(8,128)S(1)} %copy-done.2), custom_call_target="tpu_custom_call" | custom-call | tf_op jit(solution)/shard_map/pack_windows/pallas_call | solution.py:422
  14.4 0.0 copy-start.1
  14.4 1.5 %copy-done.1 = bf16[10,2,128,512]{3,2,1,0:T(8,128)(2,1)} copy-done((bf16[10,2,128,512]{3,2,1,0:T(8,128)(2,1)}, bf16[10,2,128,512]{3,2,1,0:T(8,128)(2,1)S(1)}, u32[]{:S(2)}) %copy-start.1) | copy-done | bytes 2621464
  15.9 0.0 copy-done.3
  15.9 86.6 %chain.1.got_ref = bf16[5,2,2,128,512]{4,3,2,1,0:T(8,128)(2,1)} custom-call(s32[5,8,128]{2,1,0:T(8,128)S(1)} %share_positions.1.pos_ref.row_ref, bf16[10,2,128,512]{3,2,1,0:T(8,128)(2,1)} %copy-done.1, f32[2,512,512]{2,1,0:T(8,128)} %int_ref.1, bf16[2,512,512]{2,1,0:T(8,128)(2,1)S(1)} %copy-done.3, bf16[2,512,512]{2,1,0:T(8,128)(2,1)} %prop_ref.1, ...), custom_call_target="tpu_custom_call" | custom-call | tf_op jit(solution)/shard_map/chain/pallas_call | solution.py:432
  102.5 0.0 copy-start
  102.5 1.7 %copy-done = bf16[5,2,2,128,512]{4,3,2,1,0:T(8,128)(2,1)S(1)} copy-done((bf16[5,2,2,128,512]{4,3,2,1,0:T(8,128)(2,1)S(1)}, bf16[5,2,2,128,512]{4,3,2,1,0:T(8,128)(2,1)}, u32[]{:S(2)}) %copy-start) | copy-done | bytes 2621464
  104.3 5.0 %add_gradients.1 = f32[2,1,128,2048]{3,2,1,0:T(8,128)} custom-call(s32[5,8,128]{2,1,0:T(8,128)S(1)} %share_positions.1.pos_ref.row_ref, bf16[5,2,2,128,512]{4,3,2,1,0:T(8,128)(2,1)S(1)} %copy-done), custom_call_target="tpu_custom_call" | custom-call | tf_op jit(solution)/shard_map/add_gradients/pallas_call | solution.py:460
Async XLA Ops:
  0.0 0.7 copy-start.4
  10.4 1.6 %copy-start.2 = (f32[2,1,128,2048]{3,2,1,0:T(8,128)S(1)}, f32[2,1,128,2048]{3,2,1,0:T(8,128)}, u32[]{:S(2)}) copy-start(f32[2,1,128,2048]{3,2,1,0:T(8,128)} %band.1) | copy-start | bytes 6291460
  12.0 3.9 %copy-start.3 = (bf16[2,512,512]{2,1,0:T(8,128)(2,1)S(1)}, bf16[2,512,512]{2,1,0:T(8,128)(2,1)}, u32[]{:S(2)}) copy-start(bf16[2,512,512]{2,1,0:T(8,128)(2,1)} %probe_ref.1) | copy-start | bytes 3145732
  14.4 1.5 %copy-start.1 = (bf16[10,2,128,512]{3,2,1,0:T(8,128)(2,1)}, bf16[10,2,128,512]{3,2,1,0:T(8,128)(2,1)S(1)}, u32[]{:S(2)}) copy-start(bf16[10,2,128,512]{3,2,1,0:T(8,128)(2,1)S(1)} %pack_windows.1.stage) | copy-start | bytes 7864324
  102.5 1.7 %copy-start = (bf16[5,2,2,128,512]{4,3,2,1,0:T(8,128)(2,1)S(1)}, bf16[5,2,2,128,512]{4,3,2,1,0:T(8,128)(2,1)}, u32[]{:S(2)}) copy-start(bf16[5,2,2,128,512]{4,3,2,1,0:T(8,128)(2,1)} %chain.1.got_ref) | copy-start | bytes 7864324

commit v4 on v3

--- a/solution.py
+++ b/solution.py
@@ -46,17 +46,24 @@
     return pl.multiple_of(base, LANES), column - base
 
 
-def positions_kernel(count, pos_ref, pos_out, tile, pos_in, psend, precv):
+def positions_kernel(count, pos_ref, band, pos_out, band2, pos_own, tile, pos_in, load_sem, psend, precv):
     me, cut, parity = place()
+    loads = [pltpu.make_async_copy(pos_ref, pos_own, load_sem.at[2])] + [
+        pltpu.make_async_copy(band.at[:, 0], band2.at[:, pl.ds(h * 128, 128), :], load_sem.at[h])
+        for h in range(2)
+    ]
+    for load in loads:
+        load.start()
     barrier = pltpu.get_barrier_semaphore()
     for d in range(1, REACH):
         pl.semaphore_signal(barrier, inc=1, device_id=(wrapped(me - d, count), cut), device_id_type=MESH)
+    loads[0].wait()
     lane = lax.broadcasted_iota(jnp.int32, (8, LANES), 1)
     values = jnp.zeros((8, LANES), jnp.int32)
     for n in range(4):
-        values = jnp.where(lane == n, pos_ref[n // 2, n % 2], values)
+        values = jnp.where(lane == n, pos_own[n // 2, n % 2], values)
     tile[...] = values
-    pos_out[0] = values
+    pos_out[...] = values
     pl.semaphore_wait(barrier, REACH - 1)
     copies = []
     for d in range(1, REACH):
@@ -67,27 +74,21 @@
         copies.append(copy)
     for d in range(1, REACH):
         copies[d - 1].wait()
-        pos_out[d] = pos_in[d - 1]
-
-
-def pack_kernel(pos_ref, band, stage, band2, load_sem):
+        pos_out[d:d + 1] = pos_in[d - 1, 0:1]
+    for load in loads[1:]:
+        load.wait()
+
+
+def pack_kernel(pos_ref, band2, stage):
     window = stage.shape[3]
-    width = band.shape[3]
-    loads = [
-        pltpu.make_async_copy(band.at[:, 0], band2.at[:, pl.ds(h * 128, 128), :], load_sem.at[h])
-        for h in range(2)
-    ]
-    for load in loads:
-        load.start()
-    for load in loads:
-        load.wait()
+    width = band2.shape[2]
     lane = lax.broadcasted_iota(jnp.int32, (17, 8, LANES), 2)
     sub = lax.broadcasted_iota(jnp.int32, (16, 8, LANES), 1)
     for d in range(REACH):
         for m in range(2):
-            offset = lax.rem(pos_ref[d, 0, 2 * m], 128)
+            offset = lax.rem(pos_ref[d, 2 * m], 128)
             tile_row, low_row = offset // 8, lax.rem(offset, 8)
-            base, shift = column_split(pos_ref[d, 0, 2 * m + 1], width, window)
+            base, shift = column_split(pos_ref[d, 2 * m + 1], width, window)
             turn = lax.rem(LANES - shift, LANES)
             lift = lax.rem(8 - low_row, 8)
             keep = lane + shift < LANES
@@ -106,7 +107,7 @@
 
 def chain_kernel(count, row_ref, stage, int_ref, probe_ref, prop_ref, table_ref, got,
                  win, intensity, out, edge, cross, back, prop, table,
-                 big_m, big_mt, big_f, big_ft, upright, flat, waves,
+                 bigs, bigs_t, upright, flat, waves,
                  load_sem, win_send, win_recv, self_sem, edge_send, edge_recv, cross_send, cross_self,
                  isend, irecv, out_send, out_recv, out_self, back_send, back_recv, back_self, last_send):
     me, cut, parity = place()
@@ -229,10 +230,29 @@
 
     for load in loads:
         load.wait()
+
+    def spread_out(big, re, im):
+        big[:size, :size] = re
+        big[:size, size:] = -im
+        big[size:, :size] = im
+        big[size:, size:] = re
+
+    @pl.when(active)
+    def _():
+        icopy.start()
+        upright[:size] = prop[0]
+        upright[size:] = prop[1]
+        spread_out(bigs.at[0], prop[0], prop[1])
+        spread_out(bigs_t.at[0], prop[0].T, -prop[1].T)
+        spread_out(bigs_t.at[1], table[0], table[1])
+        made = dot(bigs_t[1], upright[...]).astype(BF16)
+        spread_out(bigs.at[1], made[:size], made[size:])
+        spread_out(bigs_t.at[1], made[:size].T, -made[size:].T)
+
     for n in range(2):
         edge_copy(n).wait_recv()
     for m in range(2):
-        low = lax.broadcasted_iota(jnp.int32, (128, size), 0) < 128 - lax.rem(row_ref[2, 0, 2 * m], 128)
+        low = lax.broadcasted_iota(jnp.int32, (128, size), 0) < 128 - lax.rem(row_ref[2, 2 * m], 128)
         for part in range(2):
             cross[m, part] = jnp.where(
                 low, edge[0, m, part].astype(F32), edge[1, m, part].astype(F32)).astype(BF16)
@@ -240,19 +260,7 @@
 
     @pl.when(active)
     def _():
-        icopy.start()
-        offset = lax.rem(row_ref[2, 0, 2 * half], 128)
-        for big, big_t, src in ((big_m, big_mt, prop), (big_f, big_ft, table)):
-            re, im = src[0], src[1]
-            re_t, im_t = re.T, im.T
-            big[:size, :size] = re
-            big[:size, size:] = -im
-            big[size:, :size] = im
-            big[size:, size:] = re
-            big_t[:size, :size] = re_t
-            big_t[:size, size:] = im_t
-            big_t[size:, :size] = -im_t
-            big_t[size:, size:] = re_t
+        offset = lax.rem(row_ref[2, 2 * half], 128)
         head = lax.broadcasted_iota(jnp.int32, (128, size), 0) < 128 - offset
 
         def window_rows(s, part, e):
@@ -261,7 +269,7 @@
             low = win[s, part, after * 128:(after + 1) * 128, :].astype(F32)
             return jnp.where(head, top, low)
 
-        def forward(s, carry):
+        def enter(s):
             for e in range(4):
                 same, here = None, None
                 if e == 0:
@@ -276,33 +284,34 @@
                 p_re, p_im = waves[s, 0, rows].astype(F32), waves[s, 1, rows].astype(F32)
                 upright[rows] = (p_re * w_re - p_im * w_im).astype(BF16)
                 upright[rows_im] = (p_re * w_im + p_im * w_re).astype(BF16)
-            left(big_m)
-            made = dot(flat[...], big_mt[...])
+
+        def forward(s, carry):
+            enter(s)
+            left(bigs.at[0])
+            made = dot(flat[...], bigs_t[0])
             waves[s + 1, 0] = made[:, :size].astype(BF16)
             waves[s + 1, 1] = made[:, size:].astype(BF16)
             return carry
-        lax.fori_loop(0, slices, forward, 0)
-
-        upright[:size] = waves[slices, 0]
-        upright[size:] = waves[slices, 1]
-        left(big_f)
+        lax.fori_loop(0, slices - 1, forward, 0)
+
+        enter(slices - 1)
+        left(bigs.at[1])
         icopy.wait()
-        made = dot(flat[...], big_ft[...])
+        made = dot(flat[...], bigs_t[1])
         for e in range(4):
             rows = slice(e * 128, (e + 1) * 128)
             re, im = made[rows, :size], made[rows, size:]
             excess = re * re + im * im - intensity[rows]
-            upright[rows] = (excess * re).astype(BF16)
-            upright[size + e * 128:size + (e + 1) * 128] = (excess * im).astype(BF16)
-        left(big_ft)
-        flat[...] = dot(flat[...], big_f[...]).astype(BF16)
+            flat[rows, :size] = (excess * re).astype(BF16)
+            flat[rows, size:] = (excess * im).astype(BF16)
 
         def backward(n, carry):
             s = slices - 1 - n
-            made = dot(flat[...], big_m[...])
+            which = jnp.where(n == 0, 1, 0)
+            made = dot(flat[...], bigs[which])
             upright[:size] = made[:, :size].astype(BF16)
             upright[size:] = made[:, size:].astype(BF16)
-            made = dot(big_mt[...], upright[...])
+            made = dot(bigs_t[which], upright[...])
             terms = []
             for e in range(4):
                 rows = slice(e * 128, (e + 1) * 128)
@@ -355,12 +364,9 @@
             last_copy(m, n).wait_send()
 
 
-def add_kernel(pos_ref, got_ref, out, acc, got, load_sem):
+def add_kernel(pos_ref, got, out, acc):
     width = out.shape[3]
     window = got.shape[4]
-    loads = [pltpu.make_async_copy(got_ref.at[d], got.at[d], load_sem.at[d]) for d in range(REACH)]
-    for load in loads:
-        load.start()
     acc[...] = jnp.zeros_like(acc)
     row = 8 * lax.broadcasted_iota(jnp.int32, (16, 8, LANES), 0) + lax.broadcasted_iota(jnp.int32, (16, 8, LANES), 1)
     lane = lax.broadcasted_iota(jnp.int32, (16, 8, LANES), 2)
@@ -369,11 +375,10 @@
     zero = jnp.zeros((16, 8, LANES), F32)
     gap = jnp.zeros((1, 8, LANES), F32)
     for d in range(REACH):
-        loads[d].wait()
         for m in range(2):
-            offset = lax.rem(pos_ref[d, 0, 2 * m], 128)
+            offset = lax.rem(pos_ref[d, 2 * m], 128)
             tile_row, low_row = offset // 8, lax.rem(offset, 8)
-            base, shift = column_split(pos_ref[d, 0, 2 * m + 1], width, window)
+            base, shift = column_split(pos_ref[d, 2 * m + 1], width, window)
             turn = lax.rem(shift, LANES)
             mine = None
             if d == 0:
@@ -406,34 +411,38 @@
     vmem = pl.BlockSpec(memory_space=pltpu.VMEM)
     smem = pl.BlockSpec(memory_space=pltpu.SMEM)
     anywhere = pl.BlockSpec(memory_space=pl.ANY)
+    hbm = pl.BlockSpec(memory_space=pltpu.HBM)
     dma = pltpu.SemaphoreType.DMA
-    pos = pl.pallas_call(
+    pos, band2 = pl.pallas_call(
         functools.partial(positions_kernel, count),
-        out_shape=jax.ShapeDtypeStruct((REACH, 8, LANES), jnp.int32),
-        in_specs=[smem],
-        out_specs=vmem,
+        out_shape=[
+            jax.ShapeDtypeStruct((8, LANES), jnp.int32),
+            jax.ShapeDtypeStruct((2, 256, object_slices.shape[3]), F32),
+        ],
+        in_specs=[hbm, hbm],
+        out_specs=[vmem, vmem],
         scratch_shapes=[
-            pltpu.VMEM((8, LANES), jnp.int32), pltpu.VMEM((4, 8, LANES), jnp.int32), dma((4,)), dma((4,))],
+            pltpu.SMEM((2, 2), jnp.int32), pltpu.VMEM((8, LANES), jnp.int32), pltpu.VMEM((4, 8, LANES), jnp.int32),
+            dma((3,)), dma((4,)), dma((4,))],
         compiler_params=pltpu.CompilerParams(
-            collective_id=0, has_side_effects=True, vmem_limit_bytes=4 * 2**20),
+            collective_id=0, has_side_effects=True, vmem_limit_bytes=16 * 2**20),
         name="share_positions",
-    )(positions)
+    )(positions, object_slices)
 
     stage = pl.pallas_call(
         pack_kernel,
         out_shape=jax.ShapeDtypeStruct((10, 2, 128, size), BF16),
-        in_specs=[smem, anywhere],
+        in_specs=[smem, vmem],
         out_specs=vmem,
-        scratch_shapes=[pltpu.VMEM((2, 256, object_slices.shape[3]), F32), dma((2,))],
         compiler_params=pltpu.CompilerParams(vmem_limit_bytes=24 * 2**20),
         name="pack_windows",
-    )(pos, object_slices)
+    )(pos, band2)
 
     got = pl.pallas_call(
         functools.partial(chain_kernel, count),
         out_shape=jax.ShapeDtypeStruct((REACH, 2, 2, 128, size), BF16),
-        in_specs=[smem, vmem, anywhere, anywhere, anywhere, anywhere],
-        out_specs=anywhere,
+        in_specs=[smem, vmem, hbm, hbm, hbm, hbm],
+        out_specs=vmem,
         scratch_shapes=[
             pltpu.VMEM((4, 2, size, size), BF16),
             pltpu.VMEM((size, size), F32),
@@ -444,26 +453,25 @@
             pltpu.VMEM((2, size, size), BF16),
             pltpu.VMEM((2, size, size), BF16),
         ]
-        + [pltpu.VMEM((2 * size, 2 * size), BF16)] * 4
+        + [pltpu.VMEM((2, 2 * size, 2 * size), BF16)] * 2
         + [
             pltpu.VMEM((2 * size, size), BF16),
             pltpu.VMEM((size, 2 * size), BF16),
-            pltpu.VMEM((5, 2, size, size), BF16),
+            pltpu.VMEM((4, 2, size, size), BF16),
             dma((3,)), dma((10,)), dma((4, 4)), dma, dma((2,)), dma((2,)), dma((2,)), dma,
             dma, dma, dma((4, 4)), dma((REACH, 2)), dma, dma((4,)), dma((2,)), dma, dma((2, 2)),
         ],
         compiler_params=pltpu.CompilerParams(
-            collective_id=1, has_side_effects=True, vmem_limit_bytes=52 * 2**20),
+            collective_id=1, has_side_effects=True, vmem_limit_bytes=40 * 2**20),
         name="chain",
     )(pos, stage, intensities, probe_wave, propagator, dft_table(size))
 
     return pl.pallas_call(
         add_kernel,
         out_shape=jax.ShapeDtypeStruct(object_slices.shape, F32),
-        in_specs=[smem, anywhere],
+        in_specs=[smem, vmem],
         out_specs=vmem,
-        scratch_shapes=[
-            pltpu.VMEM((2, 256, object_slices.shape[3]), F32), pltpu.VMEM(got.shape, BF16), dma((REACH,))],
+        scratch_shapes=[pltpu.VMEM((2, 256, object_slices.shape[3]), F32)],
         compiler_params=pltpu.CompilerParams(vmem_limit_bytes=24 * 2**20),
         name="add_gradients",
     )(pos, got)

time: 110 us -> 99.3 us (0.903)
  Pallas kernels: 104 us -> 96.2 us
  local copies, waits for them, and re-layouts: 5.49 us -> 2.88 us
    pallas_call x1, Pallas kernels: 86.6 us -> 80.6 us  [local(): pl.pallas_call(functools.partial(chain_kernel, count), out_shape=jax.Shap...]
    unnamed x10 -> x12, local copies, waits for them, and re-layouts: 5.49 us -> 2.88 us
where the time goes in v4:
time: 99.3 us; the launch traced here: 99.1 us
  Pallas kernels  96.2 us (97%)
  local copies, waits for them, and re-layouts  2.88 us (3%)
    pallas_call x1, Pallas kernels, local(): pl.pallas_call(functools.partial(chain_kernel, count), out_shape=jax.Shap...  80.6 us
    pallas_call x1, Pallas kernels, local(): pl.pallas_call(functools.partial(positions_kernel, count), out_shape=[jax...  9.45 us
    pallas_call x1, Pallas kernels, local(): pl.pallas_call(add_kernel, out_shape=jax.ShapeDtypeStruct(object_slices.s...  4.3 us
    unnamed x12, local copies, waits for them, and re-layouts  2.88 us

profile of v4, /device:TPU:1, one launch (start us, length us, event | category | flops | bytes accessed | tf_op | source)
XLA Modules:
  0.0 99.1 jit_solution(554665042893472503)
XLA Ops:
  0.0 0.0 copy-start.1
  0.0 1.6 %copy-done.1 = f32[2,1,128,2048]{3,2,1,0:T(8,128)S(1)} copy-done((f32[2,1,128,2048]{3,2,1,0:T(8,128)S(1)}, f32[2,1,128,2048]{3,2,1,0:T(8,128)}, u32[]{:S(2)}) %copy-start.1) | copy-done | bytes 2097176
  1.6 0.0 copy-start.5
  1.6 0.7 copy-done.5
  2.3 9.4 %share_positions.1 = (s32[8,128]{1,0:T(8,128)S(1)}, f32[2,256,2048]{2,1,0:T(8,128)S(1)}) custom-call(s32[2,2]{1,0:T(2,128)S(1)} %copy-done.5, f32[2,1,128,2048]{3,2,1,0:T(8,128)S(1)} %copy-done.1), custom_call_target="tpu_custom_call" | custom-call | tf_op jit(solution)/shard_map/share_positions/pallas_call | solution.py:416
  11.7 0.0 copy-start
  11.7 0.0 copy-start.2
  11.8 0.0 copy-start.3
  11.8 0.0 copy-start.4
  11.8 1.8 %pack_windows.1.stage = bf16[10,2,128,512]{3,2,1,0:T(8,128)(2,1)S(1)} custom-call(s32[8,128]{1,0:T(8,128)S(1)} %get-tuple-element.7.pos_ref.row_ref, f32[2,256,2048]{2,1,0:T(8,128)S(1)} %get-tuple-element.8.band2), custom_call_target="tpu_custom_call" | custom-call | tf_op jit(solution)/shard_map/pack_windows/pallas_call | solution.py:432
  13.6 0.0 copy-done
  13.6 0.0 copy-done.2
  13.6 0.3 copy-done.3
  13.9 0.3 copy-done.4
  14.2 80.6 %chain.1.got = bf16[5,2,2,128,512]{4,3,2,1,0:T(8,128)(2,1)S(1)} custom-call(s32[8,128]{1,0:T(8,128)S(1)} %get-tuple-element.7.pos_ref.row_ref, bf16[10,2,128,512]{3,2,1,0:T(8,128)(2,1)S(1)} %pack_windows.1.stage, f32[2,512,512]{2,1,0:T(8,128)S(1)} %copy-done, bf16[2,512,512]{2,1,0:T(8,128)(2,1)S(1)} %copy-done.2, bf16[2,512,512]{2,1,0:T(8,128)(2,1)S(1)} %copy-done.3, ...), custom_call_target="tpu_custom_call" | custom-call | tf_op jit(solution)/shard_map/chain/pallas_call | solution.py:441
  94.8 4.3 %add_gradients.1 = f32[2,1,128,2048]{3,2,1,0:T(8,128)} custom-call(s32[8,128]{1,0:T(8,128)S(1)} %get-tuple-element.7.pos_ref.row_ref, bf16[5,2,2,128,512]{4,3,2,1,0:T(8,128)(2,1)S(1)} %chain.1.got), custom_call_target="tpu_custom_call" | custom-call | tf_op jit(solution)/shard_map/add_gradients/pallas_call | solution.py:469
Async XLA Ops:
  0.0 1.6 %copy-start.1 = (f32[2,1,128,2048]{3,2,1,0:T(8,128)S(1)}, f32[2,1,128,2048]{3,2,1,0:T(8,128)}, u32[]{:S(2)}) copy-start(f32[2,1,128,2048]{3,2,1,0:T(8,128)} %band.1) | copy-start | bytes 6291460
  1.6 0.7 copy-start.5
  11.7 1.9 %copy-start = (f32[2,512,512]{2,1,0:T(8,128)S(1)}, f32[2,512,512]{2,1,0:T(8,128)}, u32[]{:S(2)}) copy-start(f32[2,512,512]{2,1,0:T(8,128)} %int_ref.1) | copy-start | bytes 6291460
  11.7 1.9 %copy-start.2 = (bf16[2,512,512]{2,1,0:T(8,128)(2,1)S(1)}, bf16[2,512,512]{2,1,0:T(8,128)(2,1)}, u32[]{:S(2)}) copy-start(bf16[2,512,512]{2,1,0:T(8,128)(2,1)} %probe_ref.1) | copy-start | bytes 3145732
  11.8 2.1 %copy-start.3 = (bf16[2,512,512]{2,1,0:T(8,128)(2,1)S(1)}, bf16[2,512,512]{2,1,0:T(8,128)(2,1)}, u32[]{:S(2)}) copy-start(bf16[2,512,512]{2,1,0:T(8,128)(2,1)} %prop_ref.1) | copy-start | bytes 3145732
  11.8 2.5 %copy-start.4 = (bf16[2,512,512]{2,1,0:T(8,128)(2,1)S(1)}, bf16[2,512,512]{2,1,0:T(8,128)(2,1)}, u32[]{:S(2)}) copy-start(bf16[2,512,512]{2,1,0:T(8,128)(2,1)} %constant.2.clone.table_ref) | copy-start | bytes 3145732

commit v5 on v4

--- a/solution.py
+++ b/solution.py
@@ -46,11 +46,13 @@
     return pl.multiple_of(base, LANES), column - base
 
 
-def positions_kernel(count, pos_ref, band, pos_out, band2, pos_own, tile, pos_in, load_sem, psend, precv):
+def positions_kernel(count, pos_ref, band, pos_out, tiles, pos_own, tile, pos_in, load_sem, band_sem, psend, precv):
     me, cut, parity = place()
-    loads = [pltpu.make_async_copy(pos_ref, pos_own, load_sem.at[2])] + [
-        pltpu.make_async_copy(band.at[:, 0], band2.at[:, pl.ds(h * 128, 128), :], load_sem.at[h])
-        for h in range(2)
+    loads = [pltpu.make_async_copy(pos_ref, pos_own, load_sem)] + [
+        pltpu.make_async_copy(
+            band.at[part, :, :, pl.ds(n * LANES, LANES)], tiles.at[part, n], band_sem.at[part, n])
+        for part in range(2)
+        for n in range(tiles.shape[1])
     ]
     for load in loads:
         load.start()
@@ -79,34 +81,35 @@
         load.wait()
 
 
-def pack_kernel(pos_ref, band2, stage):
-    window = stage.shape[3]
-    width = band2.shape[2]
-    lane = lax.broadcasted_iota(jnp.int32, (17, 8, LANES), 2)
+def pack(stage, tiles, slot, row, column):
+    window, width = stage.shape[3], tiles.shape[1] * LANES
+    lane = lax.broadcasted_iota(jnp.int32, (16, 8, LANES), 2)
     sub = lax.broadcasted_iota(jnp.int32, (16, 8, LANES), 1)
-    for d in range(REACH):
-        for m in range(2):
-            offset = lax.rem(pos_ref[d, 2 * m], 128)
-            tile_row, low_row = offset // 8, lax.rem(offset, 8)
-            base, shift = column_split(pos_ref[d, 2 * m + 1], width, window)
-            turn = lax.rem(LANES - shift, LANES)
-            lift = lax.rem(8 - low_row, 8)
-            keep = lane + shift < LANES
-            keep_row = sub + low_row < 8
-            rows = pl.ds(pl.multiple_of(tile_row * 8, 8), 136)
-            for part in range(2):
-                turned = []
-                for j in range(window // LANES + 1):
-                    cols = pl.ds(pl.multiple_of(base + j * LANES, LANES), LANES)
-                    turned.append(pltpu.roll(band2[part, rows, cols].reshape(17, 8, LANES), turn, 2))
-                for j in range(window // LANES):
-                    lifted = pltpu.roll(jnp.where(keep, turned[j], turned[j + 1]), lift, 1)
-                    made = jnp.where(keep_row, lifted[:16], lifted[1:]).reshape(128, LANES)
-                    stage[d * 2 + m, part, :, j * LANES:(j + 1) * LANES] = made.astype(BF16)
-
-
-def chain_kernel(count, row_ref, stage, int_ref, probe_ref, prop_ref, table_ref, got,
-                 win, intensity, out, edge, cross, back, prop, table,
+    offset = lax.rem(row, 128)
+    tile_row, low_row = offset // 8, lax.rem(offset, 8)
+    tile_column = jnp.minimum(column // LANES, (width - window) // LANES - 1)
+    shift = column - tile_column * LANES
+    turn = lax.rem(LANES - shift, LANES)
+    lift = lax.rem(8 - low_row, 8)
+    keep = lane + shift < LANES
+    keep_row = sub + low_row < 8
+    rows = [lax.rem(tile_row + t, 16) for t in range(16)]
+
+    def one_part(part, carry):
+        turned = []
+        for j in range(window // LANES + 1):
+            turned.append(pltpu.roll(
+                jnp.stack([tiles[part, tile_column + j, rows[t]] for t in range(16)]), turn, 2))
+        for j in range(window // LANES):
+            lifted = pltpu.roll(jnp.where(keep, turned[j], turned[j + 1]), lift, 1)
+            made = jnp.where(keep_row, lifted, jnp.concatenate([lifted[1:], lifted[:1]]))
+            stage[slot, part, :, j * LANES:(j + 1) * LANES] = made.reshape(128, LANES).astype(BF16)
+        return carry
+    lax.fori_loop(0, 2, one_part, 0)
+
+
+def chain_kernel(count, row_ref, tiles, int_ref, probe_ref, prop_ref, table_ref, got,
+                 stage, win, intensity, out, edge, cross, back, prop, table,
                  bigs, bigs_t, upright, flat, waves,
                  load_sem, win_send, win_recv, self_sem, edge_send, edge_recv, cross_send, cross_self,
                  isend, irecv, out_send, out_recv, out_self, back_send, back_recv, back_self, last_send):
@@ -157,6 +160,12 @@
                 either(cut == k if d == 2 else None, lambda: greet(owner(d, k)), None)
             either(cut == k, lambda: greet(owner(2, k)), None)
 
+    def pack_all(d):
+        for m in range(2):
+            pack(stage, tiles, d * 2 + m, row_ref[d, 2 * m], row_ref[d, 2 * m + 1])
+
+    pack_all(0)
+    pack_all(4)
     pl.semaphore_wait(barrier, jnp.where(active, 22, 10))
 
     def unit(s, e):
@@ -217,6 +226,7 @@
     for n in range(2):
         edge_copy(n).start()
     for d in (1, 3, 2):
+        pack_all(d)
         for m in range(2):
             either(is_self(d, m), lambda: window_copy(d, m).start(), lambda: window_here(m).start())
 
@@ -364,16 +374,15 @@
             last_copy(m, n).wait_send()
 
 
-def add_kernel(pos_ref, got, out, acc):
+def add_kernel(pos_ref, got, out):
     width = out.shape[3]
     window = got.shape[4]
-    acc[...] = jnp.zeros_like(acc)
+    out[...] = jnp.zeros_like(out)
     row = 8 * lax.broadcasted_iota(jnp.int32, (16, 8, LANES), 0) + lax.broadcasted_iota(jnp.int32, (16, 8, LANES), 1)
     lane = lax.broadcasted_iota(jnp.int32, (16, 8, LANES), 2)
-    sub = lax.broadcasted_iota(jnp.int32, (17, 8, LANES), 1)
+    sub = lax.broadcasted_iota(jnp.int32, (16, 8, LANES), 1)
     count = window // LANES
     zero = jnp.zeros((16, 8, LANES), F32)
-    gap = jnp.zeros((1, 8, LANES), F32)
     for d in range(REACH):
         for m in range(2):
             offset = lax.rem(pos_ref[d, 2 * m], 128)
@@ -387,7 +396,7 @@
                 mine = row >= 128 - offset
             keep = lane >= shift
             keep_row = sub >= low_row
-            to_rows = pl.ds(pl.multiple_of(tile_row * 8, 8), 136)
+            to_rows = [pl.ds(pl.multiple_of(lax.rem(tile_row + t, 16) * 8, 8), 8) for t in range(16)]
             for part in range(2):
                 before = zero
                 for j in range(count + 1):
@@ -399,44 +408,36 @@
                         here = pltpu.roll(here, turn, 2)
                     moved = pltpu.roll(jnp.where(keep, here, before), low_row, 1)
                     before = here
-                    made = jnp.where(keep_row, jnp.concatenate([moved, gap]), jnp.concatenate([gap, moved]))
+                    made = jnp.where(keep_row, moved, jnp.concatenate([moved[15:], moved[:15]]))
                     to_cols = pl.ds(pl.multiple_of(base + j * LANES, LANES), LANES)
-                    acc[part, to_rows, to_cols] += made.reshape(136, LANES)
-    out[:, 0] = acc[:, :128] + acc[:, 128:]
+                    for t in range(16):
+                        out[part, 0, to_rows[t], to_cols] += made[t]
 
 
 def local(probe_wave, propagator, object_slices, positions, intensities):
     count = lax.axis_size("scan")
     size = probe_wave.shape[1]
+    columns = object_slices.shape[3] // LANES
     vmem = pl.BlockSpec(memory_space=pltpu.VMEM)
     smem = pl.BlockSpec(memory_space=pltpu.SMEM)
     anywhere = pl.BlockSpec(memory_space=pl.ANY)
     hbm = pl.BlockSpec(memory_space=pltpu.HBM)
     dma = pltpu.SemaphoreType.DMA
-    pos, band2 = pl.pallas_call(
+    pos, tiles = pl.pallas_call(
         functools.partial(positions_kernel, count),
         out_shape=[
             jax.ShapeDtypeStruct((8, LANES), jnp.int32),
-            jax.ShapeDtypeStruct((2, 256, object_slices.shape[3]), F32),
+            jax.ShapeDtypeStruct((2, columns, 16, 8, LANES), F32),
         ],
         in_specs=[hbm, hbm],
         out_specs=[vmem, vmem],
         scratch_shapes=[
             pltpu.SMEM((2, 2), jnp.int32), pltpu.VMEM((8, LANES), jnp.int32), pltpu.VMEM((4, 8, LANES), jnp.int32),
-            dma((3,)), dma((4,)), dma((4,))],
+            dma, dma((2, columns)), dma((4,)), dma((4,))],
         compiler_params=pltpu.CompilerParams(
             collective_id=0, has_side_effects=True, vmem_limit_bytes=16 * 2**20),
         name="share_positions",
-    )(positions, object_slices)
-
-    stage = pl.pallas_call(
-        pack_kernel,
-        out_shape=jax.ShapeDtypeStruct((10, 2, 128, size), BF16),
-        in_specs=[smem, vmem],
-        out_specs=vmem,
-        compiler_params=pltpu.CompilerParams(vmem_limit_bytes=24 * 2**20),
-        name="pack_windows",
-    )(pos, band2)
+    )(positions, object_slices.reshape(2, 16, 8, object_slices.shape[3]))
 
     got = pl.pallas_call(
         functools.partial(chain_kernel, count),
@@ -444,6 +445,7 @@
         in_specs=[smem, vmem, hbm, hbm, hbm, hbm],
         out_specs=vmem,
         scratch_shapes=[
+            pltpu.VMEM((10, 2, 128, size), BF16),
             pltpu.VMEM((4, 2, size, size), BF16),
             pltpu.VMEM((size, size), F32),
             pltpu.VMEM((4, 4, 2, 128, size), BF16),
@@ -464,14 +466,13 @@
         compiler_params=pltpu.CompilerParams(
             collective_id=1, has_side_effects=True, vmem_limit_bytes=40 * 2**20),
         name="chain",
-    )(pos, stage, intensities, probe_wave, propagator, dft_table(size))
+    )(pos, tiles, intensities, probe_wave, propagator, dft_table(size))
 
     return pl.pallas_call(
         add_kernel,
         out_shape=jax.ShapeDtypeStruct(object_slices.shape, F32),
         in_specs=[smem, vmem],
         out_specs=vmem,
-        scratch_shapes=[pltpu.VMEM((2, 256, object_slices.shape[3]), F32)],
         compiler_params=pltpu.CompilerParams(vmem_limit_bytes=24 * 2**20),
         name="add_gradients",
     )(pos, got)

time: 99.3 us -> 105 us (1.057)
  local copies, waits for them, and re-layouts: 2.88 us -> 5.94 us
  Pallas kernels: 96.2 us -> 98.5 us
    pallas_call x1, Pallas kernels: 4.3 us -> 8.08 us  [local(): pl.pallas_call(add_kernel, out_shape=jax.ShapeDtypeStruct(object_slices.s...]
    unnamed x12, local copies, waits for them, and re-layouts: 2.88 us -> 5.94 us
    pallas_call x1 -> x0, Pallas kernels: 1.82 us -> none  [local(): pl.pallas_call(pack_kernel, out_shape=jax.ShapeDtypeStruct((10, 2, 128, s...]
where the time goes in v5:
time: 105 us
  Pallas kernels  98.5 us (94%)
  local copies, waits for them, and re-layouts  5.94 us (6%)
    pallas_call x1, Pallas kernels, local(): pl.pallas_call(functools.partial(chain_kernel, count), out_shape=jax.Shap...  80.7 us
    pallas_call x1, Pallas kernels, local(): pl.pallas_call(functools.partial(positions_kernel, count), out_shape=[jax...  9.81 us
    pallas_call x1, Pallas kernels, local(): pl.pallas_call(add_kernel, out_shape=jax.ShapeDtypeStruct(object_slices.s...  8.08 us
    unnamed x12, local copies, waits for them, and re-layouts  5.94 us

profile of v5, /device:TPU:1, one launch (start us, length us, event | category | flops | bytes accessed | tf_op | source)
XLA Modules:
  0.0 104.5 jit_solution(12018227672386507441)
XLA Ops:
  0.0 0.0 copy-start
  0.0 1.6 %copy-done = f32[2,1,128,2048]{3,2,1,0:T(8,128)S(1)} copy-done((f32[2,1,128,2048]{3,2,1,0:T(8,128)S(1)}, f32[2,1,128,2048]{3,2,1,0:T(8,128)}, u32[]{:S(2)}) %copy-start) | copy-done | bytes 2097176
  1.6 0.0 copy-start.5
  1.6 0.7 copy-done.5
  2.3 0.0 copy-start.1
  2.3 9.8 %share_positions.1 = (s32[8,128]{1,0:T(8,128)S(1)}, f32[2,16,16,8,128]{4,3,2,1,0:T(8,128)S(1)}) custom-call(s32[2,2]{1,0:T(2,128)S(1)} %copy-done.5, f32[2,16,8,2048]{3,2,1,0:T(8,128)S(1)} %bitcast.1), custom_call_target="tpu_custom_call" | custom-call | tf_op jit(solution)/shard_map/share_positions/pallas_call | solution.py:426
  12.1 0.0 copy-done.1
  12.1 0.0 copy-start.2
  12.1 1.2 %copy-done.2 = bf16[2,512,512]{2,1,0:T(8,128)(2,1)S(1)} copy-done((bf16[2,512,512]{2,1,0:T(8,128)(2,1)S(1)}, bf16[2,512,512]{2,1,0:T(8,128)(2,1)}, u32[]{:S(2)}) %copy-start.2) | copy-done | bytes 1048600
  13.3 0.0 copy-start.3
  13.3 1.2 %copy-done.3 = bf16[2,512,512]{2,1,0:T(8,128)(2,1)S(1)} copy-done((bf16[2,512,512]{2,1,0:T(8,128)(2,1)S(1)}, bf16[2,512,512]{2,1,0:T(8,128)(2,1)}, u32[]{:S(2)}) %copy-start.3) | copy-done | bytes 1048600
  14.6 0.0 copy-start.4
  14.6 1.2 %copy-done.4 = bf16[2,512,512]{2,1,0:T(8,128)(2,1)S(1)} copy-done((bf16[2,512,512]{2,1,0:T(8,128)(2,1)S(1)}, bf16[2,512,512]{2,1,0:T(8,128)(2,1)}, u32[]{:S(2)}) %copy-start.4) | copy-done | bytes 1048600
  15.8 80.7 %chain.1.got = bf16[5,2,2,128,512]{4,3,2,1,0:T(8,128)(2,1)S(1)} custom-call(s32[8,128]{1,0:T(8,128)S(1)} %get-tuple-element.7.row_ref.pos_ref, f32[2,16,16,8,128]{4,3,2,1,0:T(8,128)S(1)} %get-tuple-element.8.tiles, f32[2,512,512]{2,1,0:T(8,128)S(1)} %copy-done.1, bf16[2,512,512]{2,1,0:T(8,128)(2,1)S(1)} %copy-done.2, bf16[2,512,512]{2,1,0:T(8,128)(2,1)S(1)} %copy-done.3, ...), custom_call_target="tpu_custom_call" | custom-call | tf_op jit(solution)/shard_map/chain/pallas_call | solution.py:442
  96.4 8.1 %add_gradients.1 = f32[2,1,128,2048]{3,2,1,0:T(8,128)} custom-call(s32[8,128]{1,0:T(8,128)S(1)} %get-tuple-element.7.row_ref.pos_ref, bf16[5,2,2,128,512]{4,3,2,1,0:T(8,128)(2,1)S(1)} %chain.1.got), custom_call_target="tpu_custom_call" | custom-call | tf_op jit(solution)/shard_map/add_gradients/pallas_call | solution.py:471
Async XLA Ops:
  0.0 1.6 %copy-start = (f32[2,1,128,2048]{3,2,1,0:T(8,128)S(1)}, f32[2,1,128,2048]{3,2,1,0:T(8,128)}, u32[]{:S(2)}) copy-start(f32[2,1,128,2048]{3,2,1,0:T(8,128)} %param.8) | copy-start | bytes 6291460
  1.6 0.7 copy-start.5
  2.3 9.8 %copy-start.1 = (f32[2,512,512]{2,1,0:T(8,128)S(1)}, f32[2,512,512]{2,1,0:T(8,128)}, u32[]{:S(2)}) copy-start(f32[2,512,512]{2,1,0:T(8,128)} %int_ref.1) | copy-start | bytes 6291460
  12.1 1.2 %copy-start.2 = (bf16[2,512,512]{2,1,0:T(8,128)(2,1)S(1)}, bf16[2,512,512]{2,1,0:T(8,128)(2,1)}, u32[]{:S(2)}) copy-start(bf16[2,512,512]{2,1,0:T(8,128)(2,1)} %probe_ref.1) | copy-start | bytes 3145732
  13.3 1.2 %copy-start.3 = (bf16[2,512,512]{2,1,0:T(8,128)(2,1)S(1)}, bf16[2,512,512]{2,1,0:T(8,128)(2,1)}, u32[]{:S(2)}) copy-start(bf16[2,512,512]{2,1,0:T(8,128)(2,1)} %prop_ref.1) | copy-start | bytes 3145732
  14.6 1.2 %copy-start.4 = (bf16[2,512,512]{2,1,0:T(8,128)(2,1)S(1)}, bf16[2,512,512]{2,1,0:T(8,128)(2,1)}, u32[]{:S(2)}) copy-start(bf16[2,512,512]{2,1,0:T(8,128)(2,1)} %constant.2.clone.table_ref) | copy-start | bytes 3145732

commit v6 on v5

--- a/solution.py
+++ b/solution.py
@@ -374,15 +374,16 @@
             last_copy(m, n).wait_send()
 
 
-def add_kernel(pos_ref, got, out):
+def add_kernel(pos_ref, got, out, acc):
     width = out.shape[3]
     window = got.shape[4]
-    out[...] = jnp.zeros_like(out)
+    acc[...] = jnp.zeros_like(acc)
     row = 8 * lax.broadcasted_iota(jnp.int32, (16, 8, LANES), 0) + lax.broadcasted_iota(jnp.int32, (16, 8, LANES), 1)
     lane = lax.broadcasted_iota(jnp.int32, (16, 8, LANES), 2)
-    sub = lax.broadcasted_iota(jnp.int32, (16, 8, LANES), 1)
+    sub = lax.broadcasted_iota(jnp.int32, (17, 8, LANES), 1)
     count = window // LANES
     zero = jnp.zeros((16, 8, LANES), F32)
+    gap = jnp.zeros((1, 8, LANES), F32)
     for d in range(REACH):
         for m in range(2):
             offset = lax.rem(pos_ref[d, 2 * m], 128)
@@ -396,7 +397,7 @@
                 mine = row >= 128 - offset
             keep = lane >= shift
             keep_row = sub >= low_row
-            to_rows = [pl.ds(pl.multiple_of(lax.rem(tile_row + t, 16) * 8, 8), 8) for t in range(16)]
+            to_rows = pl.ds(pl.multiple_of(tile_row * 8, 8), 136)
             for part in range(2):
                 before = zero
                 for j in range(count + 1):
@@ -408,10 +409,10 @@
                         here = pltpu.roll(here, turn, 2)
                     moved = pltpu.roll(jnp.where(keep, here, before), low_row, 1)
                     before = here
-                    made = jnp.where(keep_row, moved, jnp.concatenate([moved[15:], moved[:15]]))
+                    made = jnp.where(keep_row, jnp.concatenate([moved, gap]), jnp.concatenate([gap, moved]))
                     to_cols = pl.ds(pl.multiple_of(base + j * LANES, LANES), LANES)
-                    for t in range(16):
-                        out[part, 0, to_rows[t], to_cols] += made[t]
+                    acc[part, to_rows, to_cols] += made.reshape(136, LANES)
+    out[:, 0] = acc[:, :128] + acc[:, 128:]
 
 
 def local(probe_wave, propagator, object_slices, positions, intensities):
@@ -419,6 +420,10 @@
     size = probe_wave.shape[1]
     columns = object_slices.shape[3] // LANES
     vmem = pl.BlockSpec(memory_space=pltpu.VMEM)
+
+    def kept(x):
+        return pltpu.with_memory_space_constraint(x, pltpu.HBM)
+
     smem = pl.BlockSpec(memory_space=pltpu.SMEM)
     anywhere = pl.BlockSpec(memory_space=pl.ANY)
     hbm = pl.BlockSpec(memory_space=pltpu.HBM)
@@ -437,7 +442,7 @@
         compiler_params=pltpu.CompilerParams(
             collective_id=0, has_side_effects=True, vmem_limit_bytes=16 * 2**20),
         name="share_positions",
-    )(positions, object_slices.reshape(2, 16, 8, object_slices.shape[3]))
+    )(kept(positions), kept(object_slices.reshape(2, 16, 8, object_slices.shape[3])))
 
     got = pl.pallas_call(
         functools.partial(chain_kernel, count),
@@ -466,13 +471,14 @@
         compiler_params=pltpu.CompilerParams(
             collective_id=1, has_side_effects=True, vmem_limit_bytes=40 * 2**20),
         name="chain",
-    )(pos, tiles, intensities, probe_wave, propagator, dft_table(size))
+    )(pos, tiles, kept(intensities), kept(probe_wave), kept(propagator), kept(dft_table(size)))
 
     return pl.pallas_call(
         add_kernel,
         out_shape=jax.ShapeDtypeStruct(object_slices.shape, F32),
         in_specs=[smem, vmem],
         out_specs=vmem,
+        scratch_shapes=[pltpu.VMEM((2, 256, object_slices.shape[3]), F32)],
         compiler_params=pltpu.CompilerParams(vmem_limit_bytes=24 * 2**20),
         name="add_gradients",
     )(pos, got)

time: 105 us -> 94.6 us (0.901)
  local copies, waits for them, and re-layouts: 5.94 us -> 0 us
  Pallas kernels: 98.5 us -> 94.4 us
    unnamed x12 -> x0, local copies, waits for them, and re-layouts: 5.94 us -> none
    pallas_call x1, Pallas kernels: 8.08 us -> 4.3 us  [local(): pl.pallas_call(add_kernel, out_shape=jax.ShapeDtypeStruct(object_slices.s...]
where the time goes in v6:
time: 94.6 us; the launch traced here: 94.4 us
  Pallas kernels  94.4 us (100%)
    pallas_call x1, Pallas kernels, local(): pl.pallas_call(functools.partial(chain_kernel, count), out_shape=jax.Shap...  80.5 us
    pallas_call x1, Pallas kernels, local(): pl.pallas_call(functools.partial(positions_kernel, count), out_shape=[jax...  9.59 us
    pallas_call x1, Pallas kernels, local(): pl.pallas_call(add_kernel, out_shape=jax.ShapeDtypeStruct(object_slices.s...  4.3 us

profile of v6, /device:TPU:1, one launch (start us, length us, event | category | flops | bytes accessed | tf_op | source)
XLA Modules:
  0.0 94.4 jit_solution(2754898433900684854)
XLA Ops:
  0.0 9.6 %share_positions.1 = (s32[8,128]{1,0:T(8,128)S(1)}, f32[2,16,16,8,128]{4,3,2,1,0:T(8,128)S(1)}) custom-call(s32[2,2]{1,0:T(2,128)} %pos_ref.1, f32[2,16,8,2048]{3,2,1,0:T(8,128)} %bitcast.1), custom_call_target="tpu_custom_call" | custom-call | tf_op jit(solution)/shard_map/share_positions/pallas_call | solution.py:431
  9.6 80.5 %chain.1.got = bf16[5,2,2,128,512]{4,3,2,1,0:T(8,128)(2,1)S(1)} custom-call(s32[8,128]{1,0:T(8,128)S(1)} %get-tuple-element.7.row_ref.pos_ref, f32[2,16,16,8,128]{4,3,2,1,0:T(8,128)S(1)} %get-tuple-element.8.tiles, f32[2,512,512]{2,1,0:T(8,128)} %int_ref.1, bf16[2,512,512]{2,1,0:T(8,128)(2,1)} %probe_ref.1, bf16[2,512,512]{2,1,0:T(8,128)(2,1)} %prop_ref.1, ...), custom_call_target="tpu_custom_call" | custom-call | tf_op jit(solution)/shard_map/chain/pallas_call | solution.py:447
  90.1 4.3 %add_gradients.1 = f32[2,1,128,2048]{3,2,1,0:T(8,128)} custom-call(s32[8,128]{1,0:T(8,128)S(1)} %get-tuple-element.7.row_ref.pos_ref, bf16[5,2,2,128,512]{4,3,2,1,0:T(8,128)(2,1)S(1)} %chain.1.got), custom_call_target="tpu_custom_call" | custom-call | tf_op jit(solution)/shard_map/add_gradients/pallas_call | solution.py:476

commit v7 on v6

--- a/solution.py
+++ b/solution.py
@@ -48,18 +48,18 @@
 
 def positions_kernel(count, pos_ref, band, pos_out, tiles, pos_own, tile, pos_in, load_sem, band_sem, psend, precv):
     me, cut, parity = place()
-    loads = [pltpu.make_async_copy(pos_ref, pos_own, load_sem)] + [
+    barrier = pltpu.get_barrier_semaphore()
+    for d in range(1, REACH):
+        pl.semaphore_signal(barrier, inc=1, device_id=(wrapped(me - d, count), cut), device_id_type=MESH)
+    own_load = pltpu.make_async_copy(pos_ref, pos_own, load_sem)
+    own_load.start()
+    loads = [
         pltpu.make_async_copy(
             band.at[part, :, :, pl.ds(n * LANES, LANES)], tiles.at[part, n], band_sem.at[part, n])
         for part in range(2)
         for n in range(tiles.shape[1])
     ]
-    for load in loads:
-        load.start()
-    barrier = pltpu.get_barrier_semaphore()
-    for d in range(1, REACH):
-        pl.semaphore_signal(barrier, inc=1, device_id=(wrapped(me - d, count), cut), device_id_type=MESH)
-    loads[0].wait()
+    own_load.wait()
     lane = lax.broadcasted_iota(jnp.int32, (8, LANES), 1)
     values = jnp.zeros((8, LANES), jnp.int32)
     for n in range(4):
@@ -74,10 +74,12 @@
             device_id=(wrapped(me + d, count), cut), device_id_type=MESH)
         copy.start()
         copies.append(copy)
+    for load in loads:
+        load.start()
     for d in range(1, REACH):
         copies[d - 1].wait()
         pos_out[d:d + 1] = pos_in[d - 1, 0:1]
-    for load in loads[1:]:
+    for load in loads:
         load.wait()
 
 
@@ -164,8 +166,8 @@
         for m in range(2):
             pack(stage, tiles, d * 2 + m, row_ref[d, 2 * m], row_ref[d, 2 * m + 1])
 
-    pack_all(0)
-    pack_all(4)
+    for d in (0, 4, 1, 3, 2):
+        pack_all(d)
     pl.semaphore_wait(barrier, jnp.where(active, 22, 10))
 
     def unit(s, e):
@@ -226,7 +228,6 @@
     for n in range(2):
         edge_copy(n).start()
     for d in (1, 3, 2):
-        pack_all(d)
         for m in range(2):
             either(is_self(d, m), lambda: window_copy(d, m).start(), lambda: window_here(m).start())
 

time: 94.6 us -> 94.2 us (level)
  no operation moved by 1% of the time
where the time goes in v7:
time: 94.2 us; the launch traced here: 94.1 us
  Pallas kernels  94.1 us (100%)
    pallas_call x1, Pallas kernels, local(): pl.pallas_call(functools.partial(chain_kernel, count), out_shape=jax.Shap...  80.3 us
    pallas_call x1, Pallas kernels, local(): pl.pallas_call(functools.partial(positions_kernel, count), out_shape=[jax...  9.46 us
    pallas_call x1, Pallas kernels, local(): pl.pallas_call(add_kernel, out_shape=jax.ShapeDtypeStruct(object_slices.s...  4.3 us

profile of v7, /device:TPU:1, one launch (start us, length us, event | category | flops | bytes accessed | tf_op | source)
XLA Modules:
  0.0 94.1 jit_solution(9444430246516546004)
XLA Ops:
  0.0 9.5 %share_positions.1 = (s32[8,128]{1,0:T(8,128)S(1)}, f32[2,16,16,8,128]{4,3,2,1,0:T(8,128)S(1)}) custom-call(s32[2,2]{1,0:T(2,128)} %pos_ref.1, f32[2,16,8,2048]{3,2,1,0:T(8,128)} %bitcast.1), custom_call_target="tpu_custom_call" | custom-call | tf_op jit(solution)/shard_map/share_positions/pallas_call | solution.py:432
  9.5 80.3 %chain.1.got = bf16[5,2,2,128,512]{4,3,2,1,0:T(8,128)(2,1)S(1)} custom-call(s32[8,128]{1,0:T(8,128)S(1)} %get-tuple-element.7.row_ref.pos_ref, f32[2,16,16,8,128]{4,3,2,1,0:T(8,128)S(1)} %get-tuple-element.8.tiles, f32[2,512,512]{2,1,0:T(8,128)} %int_ref.1, bf16[2,512,512]{2,1,0:T(8,128)(2,1)} %probe_ref.1, bf16[2,512,512]{2,1,0:T(8,128)(2,1)} %prop_ref.1, ...), custom_call_target="tpu_custom_call" | custom-call | tf_op jit(solution)/shard_map/chain/pallas_call | solution.py:448
  89.8 4.3 %add_gradients.1 = f32[2,1,128,2048]{3,2,1,0:T(8,128)} custom-call(s32[8,128]{1,0:T(8,128)S(1)} %get-tuple-element.7.row_ref.pos_ref, bf16[5,2,2,128,512]{4,3,2,1,0:T(8,128)(2,1)S(1)} %chain.1.got), custom_call_target="tpu_custom_call" | custom-call | tf_op jit(solution)/shard_map/add_gradients/pallas_call | solution.py:477

commit v8 on v7

--- a/solution.py
+++ b/solution.py
@@ -333,7 +333,7 @@
                 for part in range(2):
                     out[s, e, part] = jnp.where(head, terms[e][part], terms[e - 1][part]).astype(BF16)
             either(cut == s, lambda: back_copy(s).start(), lambda: back_here().start())
-            for d in (1, 3, 2):
+            for d in (2, 1, 3):
                 either(cut == s if d == 2 else None,
                        lambda: block_copy(d, s).start(), lambda: block_here().start())
             for e in range(4):

time: 94.2 us -> 94.2 us (level)
  no operation moved by 1% of the time
where the time goes in v8:
time: 94.2 us; the launch traced here: 94.1 us
  Pallas kernels  94.1 us (100%)
    pallas_call x1, Pallas kernels, local(): pl.pallas_call(functools.partial(chain_kernel, count), out_shape=jax.Shap...  80.3 us
    pallas_call x1, Pallas kernels, local(): pl.pallas_call(functools.partial(positions_kernel, count), out_shape=[jax...  9.46 us
    pallas_call x1, Pallas kernels, local(): pl.pallas_call(add_kernel, out_shape=jax.ShapeDtypeStruct(object_slices.s...  4.3 us

profile of v8, /device:TPU:1, one launch (start us, length us, event | category | flops | bytes accessed | tf_op | source)
XLA Modules:
  0.0 94.1 jit_solution(8339156140905621694)
XLA Ops:
  0.0 9.5 %share_positions.1 = (s32[8,128]{1,0:T(8,128)S(1)}, f32[2,16,16,8,128]{4,3,2,1,0:T(8,128)S(1)}) custom-call(s32[2,2]{1,0:T(2,128)} %pos_ref.1, f32[2,16,8,2048]{3,2,1,0:T(8,128)} %bitcast.1), custom_call_target="tpu_custom_call" | custom-call | tf_op jit(solution)/shard_map/share_positions/pallas_call | solution.py:432
  9.5 80.3 %chain.1.got = bf16[5,2,2,128,512]{4,3,2,1,0:T(8,128)(2,1)S(1)} custom-call(s32[8,128]{1,0:T(8,128)S(1)} %get-tuple-element.7.row_ref.pos_ref, f32[2,16,16,8,128]{4,3,2,1,0:T(8,128)S(1)} %get-tuple-element.8.tiles, f32[2,512,512]{2,1,0:T(8,128)} %int_ref.1, bf16[2,512,512]{2,1,0:T(8,128)(2,1)} %probe_ref.1, bf16[2,512,512]{2,1,0:T(8,128)(2,1)} %prop_ref.1, ...), custom_call_target="tpu_custom_call" | custom-call | tf_op jit(solution)/shard_map/chain/pallas_call | solution.py:448
  89.8 4.3 %add_gradients.1 = f32[2,1,128,2048]{3,2,1,0:T(8,128)} custom-call(s32[8,128]{1,0:T(8,128)S(1)} %get-tuple-element.7.row_ref.pos_ref, bf16[5,2,2,128,512]{4,3,2,1,0:T(8,128)(2,1)S(1)} %chain.1.got), custom_call_target="tpu_custom_call" | custom-call | tf_op jit(solution)/shard_map/add_gradients/pallas_call | solution.py:477
